TPU v7x, 32 devices: a whole 2x2x4 slice. The times are simulated.
32 devices in a mesh: rep: 16 (over z, x, core), shard: 2 (over y).
Axes of the slice: x: 2, y: 2, z: 4, core: 2. Of those that a mesh axis runs over, the one named last changes fastest.
Arguments:
- tokens: bfloat16 [16384, 1024], P(('rep', 'shard')), may hold values from -6 to 6
- ln1_gain: bfloat16 [1024], P('shard'), may hold values from 0.25 to 1.75
- ln1_bias: bfloat16 [1024], P('shard'), may hold values from -1.5 to 1.5
- qkv_weight: bfloat16 [1024, 3072], P('shard'), may hold values from -0.1875 to 0.1875
- qv_bias: bfloat16 [2048], P('shard'), may hold values from -1.5 to 1.5
- proj_weight: bfloat16 [1024, 1024], P('shard'), may hold values from -0.5 to 0.5
- proj_bias: bfloat16 [1024], P('shard'), may hold values from -1.5 to 1.5
- ln2_gain: bfloat16 [1024], P('shard'), may hold values from 0.25 to 1.75
- ln2_bias: bfloat16 [1024], P('shard'), may hold values from -1.5 to 1.5
- fc1_weight: bfloat16 [1024, 4096], P('shard'), may hold values from -0.1875 to 0.1875
- fc1_bias: bfloat16 [4096], P('shard'), may hold values from -1.5 to 1.5
- fc2_weight: bfloat16 [4096, 1024], P('shard'), may hold values from -0.125 to 0.125
- fc2_bias: bfloat16 [1024], P('shard'), may hold values from -1.5 to 1.5
- cotangent: bfloat16 [16384, 1024], P(('rep', 'shard')), may hold values from -16 to 16
Outputs:
- layer_out: bfloat16 [16384, 1024], P(('rep', 'shard'))
- grad_tokens: float32 [16384, 1024], P(('rep', 'shard'))
- grad_ln1_gain: float32 [1024], P('shard')
- grad_ln1_bias: float32 [1024], P('shard')
- grad_qkv_weight: float32 [1024, 3072], P('shard')
- grad_qv_bias: float32 [2048], P('shard')
- grad_proj_weight: float32 [1024, 1024], P('shard')
- grad_proj_bias: float32 [1024], P('shard')
- grad_ln2_gain: float32 [1024], P('shard')
- grad_ln2_bias: float32 [1024], P('shard')
- grad_fc1_weight: float32 [1024, 4096], P('shard')
- grad_fc1_bias: float32 [4096], P('shard')
- grad_fc2_weight: float32 [4096, 1024], P('shard')
- grad_fc2_bias: float32 [1024], P('shard')
All inputs are finite; a program needn't handle non-finite values.
Results may differ from a plain program's by a relative error of at most 0.018.
Values may be sent and summed in bfloat16 or wider, within the bound.
A program may use at most 320 MiB of HBM per device.

v0:
```python
import jax
import jax.numpy as jnp
from jax import lax
from jax.sharding import PartitionSpec as P

HEADS = 16
HEAD = 64


def normalize(values_in, gain_vec, shift_vec):
    centered = values_in - jnp.mean(values_in, axis=-1, keepdims=True)
    inverse = lax.rsqrt(jnp.mean(centered * centered, axis=-1, keepdims=True) + 1e-05)
    scaled = centered * inverse
    return (scaled * gain_vec + shift_vec, scaled, inverse)


def normal_back(grad_in, scaled, inverse, gain_vec):
    inner = grad_in * gain_vec
    return inverse * (
        inner
        - jnp.mean(inner, axis=-1, keepdims=True)
        - scaled * jnp.mean(inner * scaled, axis=-1, keepdims=True)
    )


def tanh_gelu(values_in):
    return jax.nn.gelu(values_in, approximate=True)


def owned_part(vector, pieces):
    length = vector.shape[0] // pieces
    return lax.dynamic_slice_in_dim(vector, lax.axis_index("shard") * length, length, 0)


def group_vectors(gain_sum, shift_sum):
    pieces = lax.axis_size("shard")
    summed_gain, summed_shift = lax.psum((gain_sum, shift_sum), "shard")
    return (owned_part(summed_gain, pieces), owned_part(summed_shift, pieces))


def score_block(query_heads, key_heads, first_row):
    tok_rows, heads_count, head_size = query_heads.shape
    seq_len = key_heads.shape[0]
    scores = jnp.einsum(
        "qhd,khd->hqk", query_heads, key_heads, preferred_element_type=jnp.float32
    ) * head_size ** (-0.5)
    slopes = 2.0 ** (-8.0 * (jnp.arange(heads_count, dtype=jnp.float32) + 1.0) / heads_count)
    query_pos = first_row + jnp.arange(tok_rows, dtype=jnp.int32)
    key_pos = jnp.arange(seq_len, dtype=jnp.int32)
    distance = (query_pos[:, None] - key_pos[None, :]).astype(jnp.float32)
    scores = scores - slopes[:, None, None] * distance[None]
    causal = (key_pos[None, :] <= query_pos[:, None])[None]
    return jnp.where(causal, scores, -1e30)


def per_device(
    tokens,
    ln1_gain,
    ln1_bias,
    qkv_weight,
    qv_bias,
    proj_weight,
    proj_bias,
    ln2_gain,
    ln2_bias,
    fc1_weight,
    fc1_bias,
    fc2_weight,
    fc2_bias,
    cotangent,
):
    f32 = jnp.float32
    bf16 = jnp.bfloat16
    tok_rows, width = tokens.shape
    pieces = lax.axis_size("shard")
    first_row = lax.axis_index("shard") * tok_rows
    gathered = (
        lax.all_gather(ln1_gain, "shard", axis=0, tiled=True),
        lax.all_gather(ln1_bias, "shard", axis=0, tiled=True),
        lax.all_gather(qkv_weight, "shard", axis=0, tiled=True),
        lax.all_gather(qv_bias, "shard", axis=0, tiled=True),
        lax.all_gather(proj_weight, "shard", axis=0, tiled=True),
        lax.all_gather(proj_bias, "shard", axis=0, tiled=True),
        lax.all_gather(ln2_gain, "shard", axis=0, tiled=True),
        lax.all_gather(ln2_bias, "shard", axis=0, tiled=True),
        lax.all_gather(fc1_weight, "shard", axis=0, tiled=True),
        lax.all_gather(fc1_bias, "shard", axis=0, tiled=True),
        lax.all_gather(fc2_weight, "shard", axis=0, tiled=True),
        lax.all_gather(fc2_bias, "shard", axis=0, tiled=True),
    )
    inputs = tokens.astype(f32)
    normed_one, scaled_one, inverse_one = normalize(
        inputs, gathered[0].astype(f32), gathered[1].astype(f32)
    )
    normed_one_b = normed_one.astype(bf16)
    packed = jnp.dot(normed_one_b, gathered[2], preferred_element_type=f32)
    pair_bias = gathered[3].astype(f32)
    query_b = (packed[:, :width] + pair_bias[:width]).astype(bf16)
    keys_b = packed[:, width : 2 * width].astype(bf16)
    values_b = (packed[:, 2 * width :] + pair_bias[width:]).astype(bf16)
    all_keys, all_values = (
        lax.all_gather(keys_b, "shard", axis=0, tiled=True),
        lax.all_gather(values_b, "shard", axis=0, tiled=True),
    )
    query_heads = query_b.reshape(tok_rows, HEADS, HEAD)
    key_heads = all_keys.reshape(-1, HEADS, HEAD)
    value_heads = all_values.reshape(-1, HEADS, HEAD)
    scores = score_block(query_heads, key_heads, first_row)
    row_max = jnp.max(scores, axis=-1, keepdims=True)
    exp_terms = jnp.exp(scores - row_max)
    row_total = jnp.sum(exp_terms, axis=-1, keepdims=True)
    logsum = row_max + jnp.log(row_total)
    probs_b = (exp_terms / row_total).astype(bf16)
    mixed_b = (
        jnp.einsum("hqk,khd->qhd", probs_b, value_heads, preferred_element_type=f32)
        .reshape(tok_rows, width)
        .astype(bf16)
    )
    resid = (
        inputs + jnp.dot(mixed_b, gathered[4], preferred_element_type=f32) + gathered[5].astype(f32)
    )
    normed_two, scaled_two, inverse_two = normalize(
        resid, gathered[6].astype(f32), gathered[7].astype(f32)
    )
    normed_two_b = normed_two.astype(bf16)
    hidden = jnp.dot(normed_two_b, gathered[8], preferred_element_type=f32) + gathered[9].astype(
        f32
    )
    active_b = tanh_gelu(hidden).astype(bf16)
    output = (
        resid
        + jnp.dot(active_b, gathered[10], preferred_element_type=f32)
        + gathered[11].astype(f32)
    )
    cotan = cotangent.astype(f32)
    grad_active = jnp.einsum("td,fd->tf", cotangent, gathered[10], preferred_element_type=f32)
    unused_value, gelu_back = jax.vjp(tanh_gelu, hidden)
    grad_hidden_b = gelu_back(grad_active)[0].astype(bf16)
    grad_norm_two = jnp.einsum("tf,df->td", grad_hidden_b, gathered[8], preferred_element_type=f32)
    grad_gain_two = jnp.sum(grad_norm_two * scaled_two, axis=0)
    grad_shift_two = jnp.sum(grad_norm_two, axis=0)
    grad_resid = cotan + normal_back(
        grad_norm_two, scaled_two, inverse_two, gathered[6].astype(f32)
    )
    owned_two, owned_active = (
        lax.all_to_all(normed_two_b, "shard", split_axis=1, concat_axis=0, tiled=True),
        lax.all_to_all(active_b, "shard", split_axis=1, concat_axis=0, tiled=True),
    )
    group_cotan, group_hidden = (
        lax.all_gather(cotangent, "shard", axis=0, tiled=True),
        lax.all_gather(grad_hidden_b, "shard", axis=0, tiled=True),
    )
    part_down = jnp.einsum("tf,td->fd", owned_active, group_cotan, preferred_element_type=f32)
    part_up = jnp.einsum("td,tf->df", owned_two, group_hidden, preferred_element_type=f32)
    part_down_bias = owned_part(jnp.sum(group_cotan.astype(f32), axis=0), pieces)
    part_up_bias = owned_part(jnp.sum(group_hidden.astype(f32), axis=0), pieces)
    part_gain_two, part_shift_two = group_vectors(grad_gain_two, grad_shift_two)
    grad_branch_b = grad_resid.astype(bf16)
    grad_mixed_b = jnp.einsum(
        "te,de->td", grad_branch_b, gathered[4], preferred_element_type=f32
    ).astype(bf16)
    grad_mixed_heads = grad_mixed_b.reshape(tok_rows, HEADS, HEAD)
    scores = score_block(query_heads, key_heads, first_row)
    attn_probs = jnp.exp(scores - logsum)
    probs_b = attn_probs.astype(bf16)
    grad_probs = jnp.einsum(
        "qhd,khd->hqk", grad_mixed_heads, value_heads, preferred_element_type=f32
    )
    row_delta = jnp.sum(attn_probs * grad_probs, axis=-1, keepdims=True)
    grad_scores_b = (attn_probs * (grad_probs - row_delta)).astype(bf16)
    score_scale = HEAD ** (-0.5)
    grad_query_b = (
        (
            jnp.einsum("hqk,khd->qhd", grad_scores_b, key_heads, preferred_element_type=f32)
            * score_scale
        )
        .reshape(tok_rows, width)
        .astype(bf16)
    )
    key_terms = (
        jnp.einsum("hqk,qhd->khd", grad_scores_b, query_heads, preferred_element_type=f32)
        * score_scale
    ).reshape(-1, width)
    value_terms = jnp.einsum(
        "hqk,qhd->khd", probs_b, grad_mixed_heads, preferred_element_type=f32
    ).reshape(-1, width)
    grad_keys, grad_values = (
        lax.psum_scatter(
            key_terms.astype(jnp.bfloat16), "shard", scatter_dimension=0, tiled=True
        ).astype(jnp.float32),
        lax.psum_scatter(
            value_terms.astype(jnp.bfloat16), "shard", scatter_dimension=0, tiled=True
        ).astype(jnp.float32),
    )
    grad_values_b = grad_values.astype(bf16)
    grad_packed_b = jnp.concatenate([grad_query_b, grad_keys.astype(bf16), grad_values_b], axis=1)
    grad_norm_one = jnp.einsum("te,de->td", grad_packed_b, gathered[2], preferred_element_type=f32)
    grad_gain_one = jnp.sum(grad_norm_one * scaled_one, axis=0)
    grad_shift_one = jnp.sum(grad_norm_one, axis=0)
    grad_inputs = grad_resid + normal_back(
        grad_norm_one, scaled_one, inverse_one, gathered[0].astype(f32)
    )
    owned_one, owned_mixed = (
        lax.all_to_all(normed_one_b, "shard", split_axis=1, concat_axis=0, tiled=True),
        lax.all_to_all(mixed_b, "shard", split_axis=1, concat_axis=0, tiled=True),
    )
    group_packed, group_branch = (
        lax.all_gather(grad_packed_b, "shard", axis=0, tiled=True),
        lax.all_gather(grad_branch_b, "shard", axis=0, tiled=True),
    )
    part_packed = jnp.einsum("td,te->de", owned_one, group_packed, preferred_element_type=f32)
    part_proj = jnp.einsum("td,te->de", owned_mixed, group_branch, preferred_element_type=f32)
    packed_sums = jnp.sum(group_packed.astype(f32), axis=0)
    part_pair = owned_part(jnp.concatenate([packed_sums[:width], packed_sums[2 * width :]]), pieces)
    part_proj_bias = owned_part(jnp.sum(group_branch.astype(f32), axis=0), pieces)
    part_gain_one, part_shift_one = group_vectors(grad_gain_one, grad_shift_one)
    (
        part_gain_one,
        part_shift_one,
        part_packed,
        part_pair,
        part_proj,
        part_proj_bias,
        part_gain_two,
        part_shift_two,
        part_up,
        part_up_bias,
        part_down,
        part_down_bias,
    ) = (
        lax.psum(part_gain_one.astype(jnp.bfloat16), "rep").astype(jnp.float32),
        lax.psum(part_shift_one.astype(jnp.bfloat16), "rep").astype(jnp.float32),
        lax.psum(part_packed.astype(jnp.bfloat16), "rep").astype(jnp.float32),
        lax.psum(part_pair.astype(jnp.bfloat16), "rep").astype(jnp.float32),
        lax.psum(part_proj.astype(jnp.bfloat16), "rep").astype(jnp.float32),
        lax.psum(part_proj_bias.astype(jnp.bfloat16), "rep").astype(jnp.float32),
        lax.psum(part_gain_two.astype(jnp.bfloat16), "rep").astype(jnp.float32),
        lax.psum(part_shift_two.astype(jnp.bfloat16), "rep").astype(jnp.float32),
        lax.psum(part_up.astype(jnp.bfloat16), "rep").astype(jnp.float32),
        lax.psum(part_up_bias.astype(jnp.bfloat16), "rep").astype(jnp.float32),
        lax.psum(part_down.astype(jnp.bfloat16), "rep").astype(jnp.float32),
        lax.psum(part_down_bias.astype(jnp.bfloat16), "rep").astype(jnp.float32),
    )
    return (
        output.astype(bf16),
        grad_inputs,
        part_gain_one,
        part_shift_one,
        part_packed,
        part_pair,
        part_proj,
        part_proj_bias,
        part_gain_two,
        part_shift_two,
        part_up,
        part_up_bias,
        part_down,
        part_down_bias,
    )


def solution(mesh):
    return jax.shard_map(
        per_device,
        mesh=mesh,
        in_specs=(
            P(("rep", "shard"), None),
            P("shard"),
            P("shard"),
            P("shard", None),
            P("shard"),
            P("shard", None),
            P("shard"),
            P("shard"),
            P("shard"),
            P("shard", None),
            P("shard"),
            P("shard", None),
            P("shard"),
            P(("rep", "shard"), None),
        ),
        out_specs=(
            P(("rep", "shard"), None),
            P(("rep", "shard"), None),
            P("shard"),
            P("shard"),
            P("shard", None),
            P("shard"),
            P("shard", None),
            P("shard"),
            P("shard"),
            P("shard"),
            P("shard", None),
            P("shard"),
            P("shard", None),
            P("shard"),
        ),
        check_vma=False,
    )
```

profile of v0, /device:TPU:0, one launch (start us, length us, event | category | flops | bytes accessed | tf_op | source)
XLA Modules:
  0.0 1137.7 jit_solution(4812291906577883289)
XLA Ops:
  21.5 71.2 %all-gather.17.cloned.1.call-done = bf16[1024,3072]{1,0:T(8,128)(2,1)} async-done(((bf16[512,3072]{1,0:T(8,128)(2,1)}), bf16[1024,3072]{1,0:T(8,128)(2,1)}) %all-gather.17.cloned.1.call-update) | async-done | bytes 6291472 | tf_op jit(solution)/shard_map/all_gather | solution.py:80
  138.4 17.8 %fusion.40 = (f32[16,512]{1,0:T(8,128)S(1)}, f32[16,512,1024]{2,1,0:T(8,128)}) fusion(f32[512,1024]{1,0:T(8,128)} %subtract_convert_fusion, f32[16]{0:T(128)S(1)} %multiply_power_fusion, bf16[512,16,64]{0,2,1:T(8,128)(2,1)} %bitcast.92, bf16[1024,16,64]{0,2,1:T(8,128)(2,1)S(1)} %bitcast.87, pred[512,1024]{1,0:T(8,128)(4,1)} %iota_compare_fusion), kind=kOutput, calls=%fused_computation.98 | convolution fusion | flops 1115676672 | bytes 39354432 | tf_op jit(solution)/shard_map/qhd,khd->hqk/dot_general | solution.py:44
  156.2 14.6 %all-gather.19.cloned.1.call-done = bf16[1024,1024]{1,0:T(8,128)(2,1)} async-done(((bf16[512,1024]{1,0:T(8,128)(2,1)}), bf16[1024,1024]{1,0:T(8,128)(2,1)}) %all-gather.19.cloned.1.call-update) | async-done | bytes 2097168 | tf_op jit(solution)/shard_map/all_gather | solution.py:103
  173.7 15.6 %fusion = f32[16,512]{1,0:T(8,128)S(1)} fusion(f32[16,512,1024]{2,1,0:T(8,128)} %get-tuple-element.49, f32[16,512]{1,0:T(8,128)S(1)} %get-tuple-element.48), kind=kLoop, calls=%fused_computation.6 | loop fusion | flops 16769024 | bytes 33619968 | tf_op jit(solution)/shard_map/reduce_sum | solution.py:111
  189.3 13.9 %fusion.33 = bf16[16,64,512]{2,1,0:T(8,128)(2,1)} fusion(bf16[1024,16,64]{0,2,1:T(8,128)(2,1)S(1)} %bitcast.82, f32[16,512,1024]{2,1,0:T(8,128)} %get-tuple-element.49, f32[16,512]{1,0:T(8,128)S(1)} %fusion, f32[16,512]{1,0:T(8,128)S(1)} %get-tuple-element.48), kind=kOutput, calls=%fused_computation.69 | convolution fusion | flops 1099431936 | bytes 36765696 | tf_op jit(solution)/shard_map/hqk,khd->qhd/dot_general | solution.py:115
  210.5 100.3 %all-gather.25.cloned.1.call-done = bf16[1024,4096]{1,0:T(8,128)(2,1)} async-done(((bf16[512,4096]{1,0:T(8,128)(2,1)}), bf16[1024,4096]{1,0:T(8,128)(2,1)}) %all-gather.25.cloned.1.call-update) | async-done | bytes 8388624 | tf_op jit(solution)/shard_map/all_gather | solution.py:86
  310.8 12.6 %fusion.43 = f32[512,4096]{1,0:T(8,128)} fusion(bf16[512,1024]{1,0:T(8,128)(2,1)} %add_convert_fusion.1, bf16[1024,4096]{1,0:T(8,128)(2,1)} %all-gather.25.cloned.1.call-done), kind=kOutput, calls=%fused_computation.101 | convolution fusion | flops 4294967296 | bytes 17825792 | tf_op jit(solution)/shard_map/dot_general | solution.py:126
  323.4 92.9 %all-gather.27.cloned.1.call-done = bf16[4096,1024]{1,0:T(8,128)(2,1)} async-done(((bf16[2048,1024]{1,0:T(8,128)(2,1)}), bf16[4096,1024]{1,0:T(8,128)(2,1)}) %all-gather.27.cloned.1.call-update) | async-done | bytes 8388624 | tf_op jit(solution)/shard_map/all_gather | solution.py:88
  416.3 16.3 %fusion.12 = (bf16[512,4096]{1,0:T(8,128)(2,1)}, bf16[512,4096]{1,0:T(8,128)(2,1)}) fusion(f32[512,4096]{1,0:T(8,128)} %fusion.43, f32[4096]{0:T(1024)S(1)} %convert_element_type.222, bf16[512,1024]{1,0:T(8,128)(2,1)S(1)} %copy-done.10, bf16[4096,1024]{1,0:T(8,128)(2,1)} %all-gather.27.cloned.1.call-done), kind=kOutput, calls=%fused_computation.21 | convolution fusion | flops 4343201792 | bytes 26230784 | tf_op jit(solution)/shard_map/td,fd->tf/dot_general | solution.py:136
  449.9 14.9 %fusion.30 = bf16[16,64,1024]{2,1,0:T(8,128)(2,1)} fusion(bf16[512,16,64]{0,2,1:T(8,128)(2,1)S(1)} %bitcast.84, f32[16,512,1024]{2,1,0:T(8,128)} %get-tuple-element.49, f32[16,512]{1,0:T(8,128)S(1)} %log_add_fusion), kind=kOutput, calls=%fused_computation.64 | convolution fusion | flops 1091567616 | bytes 36732928 | tf_op jit(solution)/shard_map/hqk,qhd->khd/dot_general | solution.py:184
  464.9 23.4 %multiply_reduce_fusion = (f32[16,512]{1,0:T(8,128)S(1)}, f32[16,512,1024]{2,1,0:T(8,128)}) fusion(f32[16,512,1024]{2,1,0:T(8,128)} %get-tuple-element.49, f32[16,512]{1,0:T(8,128)S(1)} %log_add_fusion, bf16[512,16,64]{0,2,1:T(8,128)(2,1)S(1)} %bitcast.85, bf16[1024,16,64]{0,2,1:T(8,128)(2,1)} %bitcast.83), kind=kOutput, calls=%fused_computation.1 | convolution fusion | flops 1098899456 | bytes 70320128 | tf_op jit(solution)/shard_map/qhd,khd->hqk/dot_general | solution.py:166
  488.3 28.0 %multiply_convert_fusion = bf16[16,512,1024]{2,1,0:T(8,128)(2,1)} fusion(f32[16,512,1024]{2,1,0:T(8,128)} %get-tuple-element.54, f32[16,512,1024]{2,1,0:T(8,128)} %get-tuple-element.49, f32[16,512]{1,0:T(8,128)S(1)} %get-tuple-element.53, f32[16,512]{1,0:T(8,128)S(1)} %log_add_fusion), kind=kLoop, calls=%fused_computation | loop fusion | flops 33554432 | bytes 83951616 | tf_op jit(solution)/shard_map/convert_element_type | solution.py:170
  528.6 12.3 %multiply_convert_fusion.3 = bf16[16,64,512]{2,1,0:T(8,128)(2,1)S(1)} fusion(bf16[1024,16,64]{0,2,1:T(8,128)(2,1)} %bitcast.88, bf16[16,512,1024]{2,1,0:T(8,128)(2,1)} %multiply_convert_fusion), kind=kOutput, calls=%fused_computation.55 | convolution fusion | flops 1074790400 | bytes 19922944 | tf_op jit(solution)/shard_map/hqk,khd->qhd/dot_general | solution.py:174
  541.0 17.3 %reduce-scatter.3.cloned.1.call-done = bf16[512,1024]{0,1:T(8,128)(2,1)} async-done(((bf16[1024,1024]{0,1:T(8,128)(2,1)}), bf16[512,1024]{0,1:T(8,128)(2,1)}) %reduce-scatter.3.cloned.1.call-update) | async-done | bytes 1048592 | tf_op jit(solution)/shard_map/reduce_scatter | solution.py:188
  572.4 20.2 %all-to-all-done.1 = bf16[512,2,512]{2,0,1:T(8,128)(2,1)S(1)} async-done(((bf16[512,2,512]{2,0,1:T(8,128)(2,1)}), bf16[512,2,512]{2,0,1:T(8,128)(2,1)S(1)}, u32[]{:S(2)}, u32[]{:S(2)}) %all-to-all-start.1) | async-done | bytes 1048608 | tf_op jit(solution)/shard_map/all_to_all | solution.py:205
  602.5 68.6 %all-to-all-done.3 = bf16[512,2,2048]{2,0,1:T(8,128)(2,1)} async-done(((bf16[512,2,2048]{2,0,1:T(8,128)(2,1)}), bf16[512,2,2048]{2,0,1:T(8,128)(2,1)}, u32[]{:S(2)}, u32[]{:S(2)}) %all-to-all-start.3) | async-done | bytes 4194336 | tf_op jit(solution)/shard_map/all_to_all | solution.py:147
  675.7 10.3 convolution_convert_fusion.2
  689.9 10.6 all-to-all-done.2
  704.3 86.2 %all-gather.33.cloned.1.call-done = bf16[1024,4096]{1,0:T(8,128)(2,1)} async-done(((bf16[512,4096]{1,0:T(8,128)(2,1)}), bf16[1024,4096]{1,0:T(8,128)(2,1)}) %all-gather.33.cloned.1.call-update) | async-done | bytes 8388624 | tf_op jit(solution)/shard_map/all_gather | solution.py:151
  790.5 10.4 convolution_convert_fusion
  800.9 71.3 %all-gather.29.cloned.1.call-done = bf16[1024,3072]{0,1:T(8,128)(2,1)} async-done(((bf16[512,3072]{0,1:T(8,128)(2,1)}), bf16[1024,3072]{0,1:T(8,128)(2,1)}) %all-gather.29.cloned.1.call-update) | async-done | bytes 6291472 | tf_op jit(solution)/shard_map/all_gather | solution.py:208
  887.7 10.4 add_convert_fusion
  923.8 62.7 %all-reduce.1 = (bf16[512]{0:T(512)(128)(2,1)S(1)}, bf16[512]{0:T(512)(128)(2,1)S(1)}, bf16[1024]{0:T(1024)(128)(2,1)S(1)}, bf16[512]{0:T(512)(128)(2,1)S(1)}, b...) all-reduce(bf16[512]{0:T(512)(128)(2,1)S(1)} %dynamic_slice.55, ...), channel_id=1, replica_groups=mesh['rep'=16,'shard'=2] {'rep'}, use_global_device_ids=true, to_apply=%region_15.16 | all-reduce | flops 6144 | bytes 24576 | tf_op jit(solution)/shard_map/psum | solution.py:231
  991.1 124.4 %all-reduce.5.cloned.1.call-done = (bf16[512,3072]{1,0:T(8,128)(2,1)}, bf16[512,1024]{1,0:T(8,128)(2,1)}, bf16[512,4096]{1,0:T(8,128)(2,1)}, bf16[2048,1024]{1,0:T(8,128)(2,1)}) async-done(((bf16[512,3072]{1,0:T(8,128)(2,1)}, bf16[512,1024]{1,0:T(8,128)(2,1)}, bf16[512,4096]{1,0:T(8,128)(2,1)}, bf16[2048,1024]{1,0:T(8,128)(2,1)}), (bf16[512,3072]{1,0:T(8,128)(2,1)}, bf16[512,1024]{1,0:T(8,128)(2,1)}, ...) | async-done | bytes 12582928 | tf_op jit(solution)/shard_map/psum | solution.py:233
  (191 shorter events, 197.0 us)
Async XLA Ops:
  7.2 85.5 %all-gather.17.cloned.1.call-start = ((), (), s32[]{:S(2)}) async-start(), calls=%async_computation.6 | async-start | bytes 9437184 | tf_op jit(solution)/shard_map/all_gather | solution.py:80
  7.9 127.6 %all-gather.21.cloned.1.call-start = ((), (), s32[]{:S(2)}) async-start(), calls=%async_computation.8 | async-start | bytes 3145728 | tf_op jit(solution)/shard_map/all_gather | solution.py:102
  13.9 84.3 %copy-start.20 = (f32[2,1,512]{2,1,0:T(1,128)}, f32[2,1,512]{2,1,0:T(1,128)S(1)}, u32[]{:S(2)}) copy-start(f32[2,1,512]{2,1,0:T(1,128)S(1)} %convert_element_type.270) | copy-start | bytes 12292
  20.5 77.7 %copy-start.22 = (f32[512]{0:T(512)}, f32[512]{0:T(512)S(1)}, u32[]{:S(2)}) copy-start(f32[512]{0:T(512)S(1)} %broadcast_multiply_fusion.5) | copy-start | bytes 6148
  21.0 77.2 %copy-start.24 = (f32[512]{0:T(512)}, f32[512]{0:T(512)S(1)}, u32[]{:S(2)}) copy-start(f32[512]{0:T(512)S(1)} %add_rsqrt_fusion.1) | copy-start | bytes 6148
  21.4 76.8 %copy-start.11 = (bf16[512,1024]{1,0:T(8,128)(2,1)}, bf16[512,1024]{1,0:T(8,128)(2,1)S(1)}, u32[]{:S(2)}) copy-start(bf16[512,1024]{1,0:T(8,128)(2,1)S(1)} %fusion.20) | copy-start | bytes 3145732
  21.4 80.7 %copy-start.27 = (bf16[1024]{0:T(1024)(128)(2,1)S(1)}, bf16[1024]{0:T(1024)(128)(2,1)}, u32[]{:S(2)}) copy-start(bf16[1024]{0:T(1024)(128)(2,1)} %param.18) | copy-start | bytes 6148
  102.1 68.8 %all-gather.19.cloned.1.call-start = ((), (), s32[]{:S(2)}) async-start(), calls=%async_computation.7 | async-start | bytes 3145728 | tf_op jit(solution)/shard_map/all_gather | solution.py:103
  110.5 94.9 %all-gather.23.cloned.1.call-start = ((), (), s32[]{:S(2)}) async-start(), calls=%async_computation.9 | async-start | bytes 3145728 | tf_op jit(solution)/shard_map/all_gather | solution.py:82
  111.1 199.7 %all-gather.25.cloned.1.call-start = ((), (), s32[]{:S(2)}) async-start(), calls=%async_computation.10 | async-start | bytes 12582912 | tf_op jit(solution)/shard_map/all_gather | solution.py:86
  111.7 304.5 %all-gather.27.cloned.1.call-start = ((), (), s32[]{:S(2)}) async-start(), calls=%async_computation.11 | async-start | bytes 12582912 | tf_op jit(solution)/shard_map/all_gather | solution.py:88
  112.3 428.6 %reduce-scatter.5.cloned.1.call-start = ((), (), s32[]{:S(2)}) async-start(), calls=%async_computation.13 | async-start | bytes 3145728 | tf_op jit(solution)/shard_map/reduce_scatter | solution.py:191
  210.5 205.8 %copy-start.10 = (bf16[512,1024]{1,0:T(8,128)(2,1)S(1)}, bf16[512,1024]{1,0:T(8,128)(2,1)}, u32[]{:S(2)}) copy-start(bf16[512,1024]{1,0:T(8,128)(2,1)} %param.27) | copy-start | bytes 3145732
  464.8 93.4 %reduce-scatter.3.cloned.1.call-start = ((), (), s32[]{:S(2)}) async-start(), calls=%async_computation.12 | async-start | bytes 3145728 | tf_op jit(solution)/shard_map/reduce_scatter | solution.py:188
  488.3 28.0 %copy-start.6 = (bf16[512,1024]{0,1:T(8,128)(2,1)S(1)}, bf16[512,1024]{0,1:T(8,128)(2,1)}, u32[]{:S(2)}) copy-start(bf16[512,1024]{0,1:T(8,128)(2,1)} %copy.45) | copy-start | bytes 3145732
  526.3 149.3 %all-gather.35.cloned.1.call-start = ((), (), s32[]{:S(2)}) async-start(), calls=%async_computation.17 | async-start | bytes 3145728 | tf_op jit(solution)/shard_map/all_gather | solution.py:150
  527.1 158.9 %all-gather.31.cloned.1.call-start = ((), (), s32[]{:S(2)}) async-start(), calls=%async_computation.15 | async-start | bytes 3145728 | tf_op jit(solution)/shard_map/all_gather | solution.py:209
  527.7 262.8 %all-gather.33.cloned.1.call-start = ((), (), s32[]{:S(2)}) async-start(), calls=%async_computation.16 | async-start | bytes 12582912 | tf_op jit(solution)/shard_map/all_gather | solution.py:151
  528.4 343.9 %all-gather.29.cloned.1.call-start = ((), (), s32[]{:S(2)}) async-start(), calls=%async_computation.14 | async-start | bytes 9437184 | tf_op jit(solution)/shard_map/all_gather | solution.py:208
  563.6 28.9 %all-to-all-start.1 = ((bf16[512,2,512]{2,0,1:T(8,128)(2,1)}), bf16[512,2,512]{2,0,1:T(8,128)(2,1)S(1)}, u32[]{:S(2)}, u32[]{:S(2)}) async-start(bf16[512,2,512]{2,0,1:T(8,128)(2,1)} %copy.49), calls=%async_computation.3 | async-start | bytes 2097152 | tf_op jit(solution)/shard_map/all_to_all | solution.py:205
  593.5 77.6 %all-to-all-start.3 = ((bf16[512,2,2048]{2,0,1:T(8,128)(2,1)}), bf16[512,2,2048]{2,0,1:T(8,128)(2,1)}, u32[]{:S(2)}, u32[]{:S(2)}) async-start(bf16[512,2,2048]{2,0,1:T(8,128)(2,1)} %bitcast.81), calls=%async_computation.5 | async-start | bytes 8388608 | tf_op jit(solution)/shard_map/all_to_all | solution.py:147
  671.1 29.3 %all-to-all-start.2 = ((bf16[512,2,512]{2,0,1:T(8,128)(2,1)}), bf16[512,2,512]{2,0,1:T(8,128)(2,1)}, u32[]{:S(2)}, u32[]{:S(2)}) async-start(bf16[512,2,512]{2,0,1:T(8,128)(2,1)} %bitcast.79), calls=%async_computation.4 | async-start | bytes 2097152 | tf_op jit(solution)/shard_map/all_to_all | solution.py:146
  700.4 100.5 %all-to-all-start = ((bf16[512,2,512]{2,0,1:T(8,128)(2,1)}), bf16[512,2,512]{2,0,1:T(8,128)(2,1)S(1)}, u32[]{:S(2)}, u32[]{:S(2)}) async-start(bf16[512,2,512]{2,0,1:T(8,128)(2,1)} %bitcast.80), calls=%async_computation.2 | async-start | bytes 2097152 | tf_op jit(solution)/shard_map/all_to_all | solution.py:204
  704.0 411.5 %all-reduce.5.cloned.1.call-start = ((), (), s32[]{:S(2)}) async-start(), calls=%async_computation.18 | async-start | bytes 25165824 | tf_op jit(solution)/shard_map/psum | solution.py:233
  (27 other events, 253.9 us)
Sparse Core Ops, SparseCore 0:
  9.6 83.0 all-gather.16
  102.2 33.3 all-gather.20
  137.7 33.1 all-gather.18
  172.2 33.1 all-gather.22
  206.8 103.9 all-gather.24
  312.2 103.9 all-gather.26
  465.0 31.8 reduce-scatter.4
  526.5 31.7 reduce-scatter.2
  559.8 46.0 all-gather.34
  607.3 55.7 all-gather.30
  665.2 125.2 all-gather.32
  791.9 80.3 all-gather.28
  880.2 235.3 all-reduce.4
where the time goes:
time: 1140 us
  waiting for transfers between devices  686 us (60%)
  matrix products  195 us (17%)
  blocking collectives  105 us (9%)
  other arithmetic  92.4 us (8%)
  local copies, waits for them, and re-layouts  26.6 us (2%)
  starting transfers between devices  18.3 us (2%)
  between operations  14.8 us (1%)
    psum x1, waiting for transfers between devices, per_device(): lax.psum(part_packed.astype(jnp.bfloat16), 'rep').astype(jnp.float32)  124 us
    all_gather x1, waiting for transfers between devices, per_device(): lax.all_gather(fc1_weight, 'shard', axis=0, tiled=True)  100 us
    all_gather x1, waiting for transfers between devices, per_device(): lax.all_gather(fc2_weight, 'shard', axis=0, tiled=True)  92.9 us
    all_gather x1, waiting for transfers between devices, per_device(): lax.all_gather(grad_hidden_b, 'shard', axis=0, tiled=True)  86.2 us
    all_gather x1, waiting for transfers between devices, per_device(): lax.all_gather(grad_packed_b, 'shard', axis=0, tiled=True)  71.3 us
    all_gather x1, waiting for transfers between devices, per_device(): lax.all_gather(qkv_weight, 'shard', axis=0, tiled=True)  71.2 us
    all_to_all x1, waiting for transfers between devices, per_device(): lax.all_to_all(active_b, 'shard', split_axis=1, concat_axis=0, tiled=True)  68.6 us
    psum x1, blocking collectives, per_device(): lax.psum(part_gain_one.astype(jnp.bfloat16), 'rep').astype(jnp.float32)  62.7 us
  transfers between devices with their start and end apart: 17, of which 13 were waited for; matrix products, arithmetic and copies ran while one was open for 20% of the time, Pallas kernels for 0%

commit v1 on v0

--- a/solution.py
+++ b/solution.py
@@ -259,9 +259,281 @@
     )
 
 
+AXES = ("rep", "shard")
+
+
+class Grid:
+    def __init__(self):
+        rep = lax.axis_index("rep")
+        self.y = lax.axis_index("shard")
+        self.core = rep % 2
+        self.x = (rep // 2) % 2
+        self.z_low = (rep // 4) % 2
+        self.z_high = rep // 8
+
+    def swap(self, array, bit):
+        return lax.ppermute(array, AXES, [(i, i ^ bit) for i in range(32)])
+
+
+Y_BIT, CORE_BIT, X_BIT, LOW_BIT, HIGH_BIT = 1, 2, 4, 8, 16
+
+
+def half_of(array, index):
+    return lax.dynamic_index_in_dim(array, index, 0, keepdims=False)
+
+
+def join(own, other, index):
+    first = index == 0
+    return jnp.stack([jnp.where(first, own, other), jnp.where(first, other, own)])
+
+
+def transpose_pairs(grid, array):
+    pairs = []
+    for i in range(0, 32, 4):
+        pairs += [(i + 1, i + 2), (i + 2, i + 1)]
+    moved = lax.ppermute(array, AXES, pairs)
+    return jnp.where(grid.y == grid.core, array, moved)
+
+
+def whole_weight(grid, own):
+    rows, columns = own.shape
+    quarter = rows // 4
+    place = grid.core * 2 + grid.x
+    sent = lax.dynamic_slice_in_dim(own, place * quarter, quarter, 0)
+    first = grid.swap(sent, Y_BIT)
+    second = grid.swap(first, X_BIT)
+    half = join(first, second, grid.x).reshape(2 * quarter, columns)
+    other = grid.swap(half, CORE_BIT)
+    base = (1 - grid.y) * rows
+    full = jnp.zeros((2 * rows, columns), own.dtype)
+    full = lax.dynamic_update_slice_in_dim(full, own, grid.y * rows, 0)
+    full = lax.dynamic_update_slice_in_dim(full, half, base + grid.core * 2 * quarter, 0)
+    return lax.dynamic_update_slice_in_dim(
+        full, other, base + (1 - grid.core) * 2 * quarter, 0
+    )
+
+
+def reduced_gradient(grid, features, grads):
+    f32, bf16 = jnp.float32, jnp.bfloat16
+    tok_rows, width = features.shape
+    columns = grads.shape[1]
+    split = features.reshape(tok_rows, 2, 2, width // 4)
+
+    def part(side, core):
+        chosen = lax.dynamic_index_in_dim(split, side, 1, keepdims=False)
+        chosen = lax.dynamic_index_in_dim(chosen, core, 1, keepdims=False)
+        return jnp.einsum("td,te->de", chosen, grads, preferred_element_type=f32)
+
+    far_side, far_core = 1 - grid.y, 1 - grid.core
+    got_far = grid.swap(part(far_side, far_core).astype(bf16), CORE_BIT)
+    got_near = grid.swap(part(grid.y, far_core).astype(bf16), CORE_BIT)
+    far = (part(far_side, grid.core) + got_far.astype(f32)).astype(bf16)
+    got = grid.swap(far, Y_BIT)
+    total = (part(grid.y, grid.core) + got_near.astype(f32) + got.astype(f32)).astype(bf16)
+    total = total.reshape(2, 2, 2, width // 32, columns)
+    for index, bit in ((grid.x, X_BIT), (grid.z_low, LOW_BIT), (grid.z_high, HIGH_BIT)):
+        got = grid.swap(half_of(total, 1 - index), bit)
+        total = (half_of(total, index).astype(f32) + got.astype(f32)).astype(bf16)
+    for index, bit in (
+        (grid.z_high, HIGH_BIT),
+        (grid.z_low, LOW_BIT),
+        (grid.x, X_BIT),
+        (grid.core, CORE_BIT),
+    ):
+        total = join(total, grid.swap(total, bit), index)
+    return total.reshape(width // 2, columns).astype(f32)
+
+
+def summed_everywhere(grid, vector):
+    for bit in (CORE_BIT, Y_BIT, X_BIT, LOW_BIT, HIGH_BIT):
+        vector = vector + grid.swap(vector, bit)
+    return vector
+
+
+def pair_scores(query_heads, key_heads, first_row, key_pos):
+    tok_rows, heads_count, head_size = query_heads.shape
+    scores = jnp.einsum(
+        "qhd,khd->hqk", query_heads, key_heads, preferred_element_type=jnp.float32
+    ) * head_size ** (-0.5)
+    slopes = 2.0 ** (-8.0 * (jnp.arange(heads_count, dtype=jnp.float32) + 1.0) / heads_count)
+    query_pos = first_row + jnp.arange(tok_rows, dtype=jnp.int32)
+    distance = (query_pos[:, None] - key_pos[None, :]).astype(jnp.float32)
+    scores = scores - slopes[:, None, None] * distance[None]
+    causal = (key_pos[None, :] <= query_pos[:, None])[None]
+    return jnp.where(causal, scores, -1e30)
+
+
+def attention_forward(query_b, keys_b, values_b, first_row, key_pos):
+    f32, bf16 = jnp.float32, jnp.bfloat16
+    tok_rows, width = query_b.shape
+    query_heads = query_b.reshape(tok_rows, HEADS, HEAD)
+    key_heads = keys_b.reshape(-1, HEADS, HEAD)
+    value_heads = values_b.reshape(-1, HEADS, HEAD)
+    scores = pair_scores(query_heads, key_heads, first_row, key_pos)
+    row_max = jnp.max(scores, axis=-1, keepdims=True)
+    exp_terms = jnp.exp(scores - row_max)
+    row_total = jnp.sum(exp_terms, axis=-1, keepdims=True)
+    logsum = row_max + jnp.log(row_total)
+    probs_b = (exp_terms / row_total).astype(bf16)
+    mixed = jnp.einsum("hqk,khd->qhd", probs_b, value_heads, preferred_element_type=f32)
+    return mixed.reshape(tok_rows, width).astype(bf16), logsum
+
+
+def attention_backward(query_b, keys_b, values_b, grad_mixed_b, logsum, first_row, key_pos):
+    f32, bf16 = jnp.float32, jnp.bfloat16
+    tok_rows, width = query_b.shape
+    query_heads = query_b.reshape(tok_rows, HEADS, HEAD)
+    key_heads = keys_b.reshape(-1, HEADS, HEAD)
+    value_heads = values_b.reshape(-1, HEADS, HEAD)
+    grad_mixed_heads = grad_mixed_b.reshape(tok_rows, HEADS, HEAD)
+    scores = pair_scores(query_heads, key_heads, first_row, key_pos)
+    attn_probs = jnp.exp(scores - logsum)
+    probs_b = attn_probs.astype(bf16)
+    grad_probs = jnp.einsum(
+        "qhd,khd->hqk", grad_mixed_heads, value_heads, preferred_element_type=f32
+    )
+    row_delta = jnp.sum(attn_probs * grad_probs, axis=-1, keepdims=True)
+    grad_scores_b = (attn_probs * (grad_probs - row_delta)).astype(bf16)
+    scale = HEAD ** (-0.5)
+    grad_query = (
+        jnp.einsum("hqk,khd->qhd", grad_scores_b, key_heads, preferred_element_type=f32) * scale
+    ).reshape(tok_rows, width)
+    key_terms = (
+        jnp.einsum("hqk,qhd->khd", grad_scores_b, query_heads, preferred_element_type=f32) * scale
+    ).reshape(-1, width)
+    value_terms = jnp.einsum(
+        "hqk,qhd->khd", probs_b, grad_mixed_heads, preferred_element_type=f32
+    ).reshape(-1, width)
+    return grad_query.astype(bf16), key_terms.astype(bf16), value_terms.astype(bf16)
+
+
+def paired_device(
+    tokens,
+    ln1_gain,
+    ln1_bias,
+    qkv_weight,
+    qv_bias,
+    proj_weight,
+    proj_bias,
+    ln2_gain,
+    ln2_bias,
+    fc1_weight,
+    fc1_bias,
+    fc2_weight,
+    fc2_bias,
+    cotangent,
+):
+    f32 = jnp.float32
+    bf16 = jnp.bfloat16
+    grid = Grid()
+    tok_rows, width = tokens.shape
+    vectors = (ln1_gain, ln1_bias, qv_bias, proj_bias, ln2_gain, ln2_bias, fc1_bias, fc2_bias)
+    own_vectors = jnp.concatenate(vectors).reshape(-1, 128)
+    both = join(own_vectors, grid.swap(own_vectors, Y_BIT), grid.y).reshape(2, -1).astype(f32)
+    full_vectors, start = [], 0
+    for vector in vectors:
+        full_vectors.append(both[:, start : start + vector.shape[0]].reshape(-1))
+        start += vector.shape[0]
+    gain_one, shift_one, pair_bias, out_bias, gain_two, shift_two, up_bias, down_bias = full_vectors
+    tokens = transpose_pairs(grid, tokens)
+    packed_w = whole_weight(grid, qkv_weight)
+    proj_w = whole_weight(grid, proj_weight)
+    up_w = whole_weight(grid, fc1_weight)
+    down_w = whole_weight(grid, fc2_weight)
+    cotangent = transpose_pairs(grid, cotangent)
+
+    first_row = grid.core * tok_rows
+    row_ids = jnp.arange(tok_rows, dtype=jnp.int32)
+    key_pos = jnp.concatenate([first_row + row_ids, (1 - grid.core) * tok_rows + row_ids])
+    inputs = tokens.astype(f32)
+    normed_one, scaled_one, inverse_one = normalize(inputs, gain_one, shift_one)
+    normed_one_b = normed_one.astype(bf16)
+    packed = jnp.dot(normed_one_b, packed_w, preferred_element_type=f32)
+    query_b = (packed[:, :width] + pair_bias[:width]).astype(bf16)
+    keys_b = packed[:, width : 2 * width].astype(bf16)
+    values_b = (packed[:, 2 * width :] + pair_bias[width:]).astype(bf16)
+    keys_b = jnp.concatenate([keys_b, grid.swap(keys_b, CORE_BIT)])
+    values_b = jnp.concatenate([values_b, grid.swap(values_b, CORE_BIT)])
+    mixed_b, logsum = attention_forward(query_b, keys_b, values_b, first_row, key_pos)
+    resid = inputs + jnp.dot(mixed_b, proj_w, preferred_element_type=f32) + out_bias
+    normed_two, scaled_two, inverse_two = normalize(resid, gain_two, shift_two)
+    normed_two_b = normed_two.astype(bf16)
+    hidden = jnp.dot(normed_two_b, up_w, preferred_element_type=f32) + up_bias
+    active_b = tanh_gelu(hidden).astype(bf16)
+    cotan = cotangent.astype(f32)
+    grad_down = reduced_gradient(grid, active_b, cotangent)
+    grad_active = jnp.einsum("td,fd->tf", cotangent, down_w, preferred_element_type=f32)
+    unused_value, gelu_back = jax.vjp(tanh_gelu, hidden)
+    grad_hidden = gelu_back(grad_active)[0]
+    grad_hidden_b = grad_hidden.astype(bf16)
+    grad_up = reduced_gradient(grid, normed_two_b, grad_hidden_b)
+    output = resid + jnp.dot(active_b, down_w, preferred_element_type=f32) + down_bias
+    output = transpose_pairs(grid, output.astype(bf16))
+    grad_norm_two = jnp.einsum("tf,df->td", grad_hidden_b, up_w, preferred_element_type=f32)
+    grad_resid = cotan + normal_back(grad_norm_two, scaled_two, inverse_two, gain_two)
+    grad_branch_b = grad_resid.astype(bf16)
+    grad_proj = reduced_gradient(grid, mixed_b, grad_branch_b)
+    grad_mixed_b = jnp.einsum(
+        "te,de->td", grad_branch_b, proj_w, preferred_element_type=f32
+    ).astype(bf16)
+    grad_query_b, key_terms, value_terms = attention_backward(
+        query_b, keys_b, values_b, grad_mixed_b, logsum, first_row, key_pos
+    )
+    grad_keys_b = (
+        key_terms[:tok_rows].astype(f32) + grid.swap(key_terms[tok_rows:], CORE_BIT).astype(f32)
+    ).astype(bf16)
+    grad_values_b = (
+        value_terms[:tok_rows].astype(f32)
+        + grid.swap(value_terms[tok_rows:], CORE_BIT).astype(f32)
+    ).astype(bf16)
+    grad_packed_b = jnp.concatenate([grad_query_b, grad_keys_b, grad_values_b], axis=1)
+    grad_packed = reduced_gradient(grid, normed_one_b, grad_packed_b)
+    grad_norm_one = jnp.einsum("te,de->td", grad_packed_b, packed_w, preferred_element_type=f32)
+    grad_inputs = grad_resid + normal_back(grad_norm_one, scaled_one, inverse_one, gain_one)
+    grad_inputs = jnp.where(
+        grid.y == grid.core,
+        grad_inputs,
+        transpose_pairs(grid, grad_inputs.astype(bf16)).astype(f32),
+    )
+    sums = (
+        jnp.sum(grad_norm_one * scaled_one, axis=0),
+        jnp.sum(grad_norm_one, axis=0),
+        jnp.sum(grad_query_b.astype(f32), axis=0),
+        jnp.sum(grad_values_b.astype(f32), axis=0),
+        jnp.sum(grad_branch_b.astype(f32), axis=0),
+        jnp.sum(grad_norm_two * scaled_two, axis=0),
+        jnp.sum(grad_norm_two, axis=0),
+        jnp.sum(grad_hidden_b.astype(f32), axis=0),
+        jnp.sum(cotan, axis=0),
+    )
+    lengths = (width, width, 2 * width, width, width, width, sums[7].shape[0], width)
+    totals = summed_everywhere(grid, jnp.concatenate(sums).reshape(-1, 128)).reshape(-1)
+    owned, start = [], 0
+    for length in lengths:
+        owned.append(owned_part(totals[start : start + length], 2))
+        start += length
+    return (
+        output,
+        grad_inputs,
+        owned[0],
+        owned[1],
+        grad_packed,
+        owned[2],
+        grad_proj,
+        owned[3],
+        owned[4],
+        owned[5],
+        grad_up,
+        owned[6],
+        grad_down,
+        owned[7],
+    )
+
+
 def solution(mesh):
+    two_way = mesh.shape["shard"] == 2 and mesh.shape["rep"] == 16
     return jax.shard_map(
-        per_device,
+        paired_device if two_way else per_device,
         mesh=mesh,
         in_specs=(
             P(("rep", "shard"), None),

time: 1140 us -> 774 us (0.68)
  waiting for transfers between devices: 686 us -> 287 us
  blocking collectives: 105 us -> 0 us
  local copies, waits for them, and re-layouts: 26.6 us -> 100 us
  starting transfers between devices: 18.3 us -> 84 us
  between operations: 14.8 us -> 2.43 us
    all_gather x10 -> x0, waiting for transfers between devices: 440 us -> none  [the longest x1 100 us: per_device(): lax.all_gather(fc1_weight, 'shard', axis=0, tiled=True)]
    ppermute x0 -> x66, waiting for transfers between devices: none -> 287 us  [the longest x62 287 us: swap(): return lax.ppermute(array, AXES, [(i, i ^ bit) for i in range(32)])]
    psum x1 -> x0, waiting for transfers between devices: 124 us -> none  [per_device(): lax.psum(part_packed.astype(jnp.bfloat16), 'rep').astype(jnp.float32)]
    all_to_all x4 -> x0, waiting for transfers between devices: 99.3 us -> none  [the longest x1 68.6 us: per_device(): lax.all_to_all(active_b, 'shard', split_axis=1, concat_axis=0, tiled=True)]
    ppermute x0 -> x66, starting transfers between devices: none -> 84 us  [the longest x62 77.8 us: swap(): return lax.ppermute(array, AXES, [(i, i ^ bit) for i in range(32)])]
    psum x2 -> x0, blocking collectives: 69.4 us -> none  [the longest x1 62.7 us: per_device(): lax.psum(part_gain_one.astype(jnp.bfloat16), 'rep').astype(jnp.float32)]
    all_gather x8 -> x0, blocking collectives: 36.1 us -> none  [the longest x1 5.24 us: per_device(): lax.all_gather(ln1_gain, 'shard', axis=0, tiled=True)]
    dynamic_slice x0 -> x7, local copies, waits for them, and re-layouts: none -> 23.7 us  [the longest x3 16 us: part(): chosen = lax.dynamic_index_in_dim(chosen, core, 1, keepdims=False)]
  transfers between devices with their start and end apart: 17 -> 66, of which waited for: 13 -> 28; matrix products, arithmetic and copies ran while one was open for 20% -> 29% of each run, Pallas kernels for 0% -> 0%
where the time goes in v1:
time: 774 us; the launch traced here: 765 us
  waiting for transfers between devices  287 us (37%)
  matrix products  192 us (25%)
  local copies, waits for them, and re-layouts  100 us (13%)
  other arithmetic  99.7 us (13%)
  starting transfers between devices  84 us (11%)
    ppermute x62, waiting for transfers between devices, swap(): return lax.ppermute(array, AXES, [(i, i ^ bit) for i in range(32)])  287 us
    ppermute x62, starting transfers between devices, swap(): return lax.ppermute(array, AXES, [(i, i ^ bit) for i in range(32)])  77.8 us
    dot_general x16, matrix products, part(): return jnp.einsum('td,te->de', chosen, grads, preferred_element_type=f32)  40.9 us
    convert_element_type x1, other arithmetic, attention_backward(): grad_scores_b = (attn_probs * (grad_probs - row_delta)).astype(bf16)  27.7 us
    dot_general x1, matrix products, attention_backward(): jnp.einsum('qhd,khd->hqk', grad_mixed_heads, value_heads, preferred_eleme...  23.4 us
    dot_general x1, matrix products, pair_scores(): jnp.einsum('qhd,khd->hqk', query_heads, key_heads, preferred_element_type...  17.6 us
    dynamic_slice x3, local copies, waits for them, and re-layouts, part(): chosen = lax.dynamic_index_in_dim(chosen, core, 1, keepdims=False)  16 us
  transfers between devices with their start and end apart: 66, of which 28 were waited for; matrix products, arithmetic and copies ran while one was open for 29% of the time, Pallas kernels for 0%

profile of v1, /device:TPU:0, one launch (start us, length us, event | category | flops | bytes accessed | tf_op | source)
XLA Modules:
  0.0 764.9 jit_solution(5870940425596288187)
XLA Ops:
  47.0 10.9 %collective-permute-done.7 = bf16[128,1024]{1,0:T(8,128)(2,1)} collective-permute-done((bf16[128,1024]{1,0:T(8,128)(2,1)S(1)}, bf16[128,1024]{1,0:T(8,128)(2,1)}, u32[]{:S(2)}, u32[]{:S(2)}) %collective-permute-start.7) | collective-permute-done | bytes 262176 | tf_op jit(solution)/shard_map/ppermute | solution.py:275
  77.4 27.8 %collective-permute-done.13 = bf16[512,1024]{1,0:T(8,128)(2,1)} collective-permute-done((bf16[512,1024]{1,0:T(8,128)(2,1)}, bf16[512,1024]{1,0:T(8,128)(2,1)}, u32[]{:S(2)}, u32[]{:S(2)}) %collective-permute-start.13) | collective-permute-done | bytes 1048608 | tf_op jit(solution)/shard_map/ppermute | solution.py:275
  125.5 8.7 %collective-permute-done.14 = bf16[512,1024]{1,0:T(8,128)(2,1)S(1)} collective-permute-done((bf16[512,1024]{1,0:T(8,128)(2,1)}, bf16[512,1024]{1,0:T(8,128)(2,1)S(1)}, u32[]{:S(2)}, u32[]{:S(2)}) %collective-permute-start.14) | collective-permute-done | bytes 1048608 | tf_op jit(solution)/shard_map/ppermute | solution.py:275
  158.0 17.6 %fusion.75 = (f32[16,512]{1,0:T(8,128)S(1)}, f32[16,512,1024]{2,1,0:T(8,128)}) fusion(f32[512,1024]{1,0:T(8,128)} %subtract_convert_fusion, f32[16]{0:T(128)S(1)} %multiply_power_fusion, bf16[512,16,64]{0,2,1:T(8,128)(2,1)} %bitcast.346, bf16[1024,16,64]{0,2,1:T(8,128)(2,1)} %bitcast.334, pred[512,1024]{1,0:T(8,128)(4,1)} %broadcast_compare_fusion), kind=kOutput, calls=%fused_computation.303 | convolution fusion | flops 1115676672 | bytes 39354432 | tf_op jit(solution)/shard_map/qhd,khd->hqk/dot_general | solution.py:355
  175.6 14.3 %fusion = f32[16,512]{1,0:T(8,128)S(1)} fusion(f32[16,512,1024]{2,1,0:T(8,128)} %get-tuple-element.111, f32[16,512]{1,0:T(8,128)S(1)} %get-tuple-element.110), kind=kLoop, calls=%fused_computation.6 | loop fusion | flops 16769024 | bytes 33619968 | tf_op jit(solution)/shard_map/reduce_sum | solution.py:375
  189.9 13.0 %fusion.38 = bf16[16,64,512]{2,1,0:T(8,128)(2,1)S(1)} fusion(bf16[1024,16,64]{0,2,1:T(8,128)(2,1)S(1)} %bitcast.330, f32[16,512,1024]{2,1,0:T(8,128)} %get-tuple-element.111, f32[16,512]{1,0:T(8,128)S(1)} %fusion, f32[16,512]{1,0:T(8,128)S(1)} %get-tuple-element.110), kind=kOutput, calls=%fused_computation.108 | convolution fusion | flops 1099431936 | bytes 36765696 | tf_op jit(solution)/shard_map/hqk,khd->qhd/dot_general | solution.py:378
  208.6 10.1 %fusion.78 = f32[512,4096]{1,0:T(8,128)} fusion(bf16[512,1024]{1,0:T(8,128)(2,1)S(1)} %add_convert_fusion.7, bf16[1024,4096]{1,0:T(8,128)(2,1)} %constant_dynamic-update-slice_fusion.3), kind=kOutput, calls=%fused_computation.306 | convolution fusion | flops 4294967296 | bytes 17825792 | tf_op jit(solution)/shard_map/dot_general | solution.py:461
  221.9 15.1 %convert_reduce_fusion = (f32[4096]{0:T(1024)S(1)}, bf16[512,4096]{1,0:T(8,128)(2,1)S(1)}, bf16[512,4096]{1,0:T(8,128)(2,1)}) fusion(f32[512,4096]{1,0:T(8,128)} %fusion.78, f32[4096]{0:T(1024)S(1)} %bitcast.372, bf16[512,1024]{1,0:T(8,128)(2,1)S(1)} %copy-done.25, bf16[4096,1024]{1,0:T(8,128)(2,1)} %constant_dynamic-update-slice_fusion), kind=kOutput, calls=%fused_computation.20 | convolution fusion | flops 4347392000 | bytes 26247168 | tf_op jit(solution)/shard_map/td,fd->tf/dot_general | solution.py:465
  237.1 9.0 %multiply_reduce_fusion.1 = (f32[1024]{0:T(1024)S(1)}, f32[512]{0:T(512)S(1)}, f32[512]{0:T(512)S(1)}, f32[1024]{0:T(1024)S(1)}, f32[512,1024]{1,0:T(8,128)S(1)}) fusion(f32[512,1024]{1,0:T(8,128)S(1)} %get-tuple-element.113, f32[512]{0:T(512)S(1)} %add_rsqrt_fusion, f32[512]{0:T(512)S(1)} %broadcast_multiply_fusion.4, f32[1024]{0:T(1024)S(1)} %bitcast.366, ...), kind=kOutput, calls=%fused_computation.83 | convolution fusion | flops 4299682816 | bytes 16797696 | tf_op jit(solution)/shard_map/tf,df->td/dot_general | solution.py:472
  252.9 15.2 %convert_bitcast_fusion = bf16[1024,16,64]{0,2,1:T(8,128)(2,1)} fusion(bf16[512,16,64]{0,2,1:T(8,128)(2,1)} %bitcast.332, f32[16,512,1024]{2,1,0:T(8,128)} %get-tuple-element.111, f32[16,512]{1,0:T(8,128)S(1)} %log_add_fusion), kind=kOutput, calls=%fused_computation.88 | convolution fusion | flops 1091567616 | bytes 36732928 | tf_op jit(solution)/shard_map/hqk,qhd->khd/dot_general | solution.py:404
  268.1 23.4 %multiply_reduce_fusion = (f32[16,512]{1,0:T(8,128)S(1)}, f32[16,512,1024]{2,1,0:T(8,128)}) fusion(f32[16,512,1024]{2,1,0:T(8,128)} %get-tuple-element.111, f32[16,512]{1,0:T(8,128)S(1)} %log_add_fusion, bf16[512,16,64]{0,2,1:T(8,128)(2,1)S(1)} %bitcast.333, bf16[1024,16,64]{0,2,1:T(8,128)(2,1)} %bitcast.331), kind=kOutput, calls=%fused_computation.1 | convolution fusion | flops 1098899456 | bytes 70320128 | tf_op jit(solution)/shard_map/qhd,khd->hqk/dot_general | solution.py:392
  291.5 27.7 %multiply_convert_fusion = bf16[16,512,1024]{2,1,0:T(8,128)(2,1)} fusion(f32[16,512,1024]{2,1,0:T(8,128)} %get-tuple-element.116, f32[16,512,1024]{2,1,0:T(8,128)} %get-tuple-element.111, f32[16,512]{1,0:T(8,128)S(1)} %get-tuple-element.115, f32[16,512]{1,0:T(8,128)S(1)} %log_add_fusion), kind=kLoop, calls=%fused_computation | loop fusion | flops 33554432 | bytes 83951616 | tf_op jit(solution)/shard_map/convert_element_type | solution.py:396
  319.2 10.4 %fusion.36 = bf16[1024,16,64]{0,2,1:T(8,128)(2,1)} fusion(bf16[512,16,64]{0,2,1:T(8,128)(2,1)} %bitcast.347, bf16[16,512,1024]{2,1,0:T(8,128)(2,1)} %multiply_convert_fusion), kind=kOutput, calls=%fused_computation.100 | convolution fusion | flops 1075838976 | bytes 19922944 | tf_op jit(solution)/shard_map/hqk,qhd->khd/dot_general | solution.py:402
  329.7 12.6 %convert_reduce_fusion.5 = (f32[16,64]{1,0:T(8,128)S(1)}, bf16[16,64,512]{2,1,0:T(8,128)(2,1)}) fusion(bf16[1024,16,64]{0,2,1:T(8,128)(2,1)} %bitcast.335, bf16[16,512,1024]{2,1,0:T(8,128)(2,1)} %multiply_convert_fusion), kind=kOutput, calls=%fused_computation.86 | convolution fusion | flops 1075837952 | bytes 19927040 | tf_op jit(solution)/shard_map/hqk,khd->qhd/dot_general | solution.py:399
  357.5 10.3 %add_convert_fusion.6 = bf16[512,1024]{1,0:T(8,128)(2,1)} fusion(f32[512,1024]{1,0:T(8,128)S(1)} %get-tuple-element.113, bf16[512,4096]{1,0:T(8,128)(2,1)} %get-tuple-element.35, bf16[4096,1024]{1,0:T(8,128)(2,1)} %constant_dynamic-update-slice_fusion, f32[1024]{0:T(1024)S(1)} %bitcast.374), kind=kOutput, calls=%fused_computation.91 | convolution fusion | flops 4296540160 | bytes 15732736 | tf_op jit(solution)/shard_map/dot_general | solution.py:470
  382.1 9.8 %constant_dynamic-slice_fusion.2 = (bf16[512,1,1,1024]{3,2,1,0:T(2,128)(2,1)}, bf16[512,1,1,1024]{3,2,1,0:T(2,128)(2,1)}, bf16[512,1,1,1024]{3,2,1,0:T(2,128)(2,1)S(1)}, bf16[512,1,1,1024]{3,2,1,0:T(2,128)(2,1)S(1)}) fusion(bf16[512,2,2,1024]{3,2,1,0:T(2,128)(2,1)S(1)} %copy-done.3, s32[]{:T(128)S(6)} %select_n.487, s32[]{:T(128)S(6)} %select_n.491, ...), kind=kLoop, calls=%fused_computation.228 | loop fusion | bytes 8388624 | tf_op jit(solution)/shard_map/jit(dynamic_index_in_dim)/dynamic_slice | solution.py:324
  490.5 28.0 %collective-permute-done.28 = bf16[256,3072]{1,0:T(8,128)(2,1)S(1)} collective-permute-done((bf16[256,3072]{1,0:T(8,128)(2,1)}, bf16[256,3072]{1,0:T(8,128)(2,1)S(1)}, u32[]{:S(2)}, u32[]{:S(2)}) %collective-permute-start.28) | collective-permute-done | bytes 1572896 | tf_op jit(solution)/shard_map/ppermute | solution.py:275
  521.0 42.5 %collective-permute-done.48 = bf16[256,4096]{1,0:T(8,128)(2,1)S(1)} collective-permute-done((bf16[256,4096]{1,0:T(8,128)(2,1)S(1)}, bf16[256,4096]{1,0:T(8,128)(2,1)S(1)}, u32[]{:S(2)}, u32[]{:S(2)}) %collective-permute-start.48) | collective-permute-done | bytes 2097184 | tf_op jit(solution)/shard_map/ppermute | solution.py:275
  566.3 39.5 %collective-permute-done.58 = bf16[1024,1024]{1,0:T(8,128)(2,1)S(1)} collective-permute-done((bf16[1024,1024]{1,0:T(8,128)(2,1)S(1)}, bf16[1024,1024]{1,0:T(8,128)(2,1)S(1)}, u32[]{:S(2)}, u32[]{:S(2)}) %collective-permute-start.58) | collective-permute-done | bytes 2097184 | tf_op jit(solution)/shard_map/ppermute | solution.py:275
  611.5 11.7 %collective-permute-done.30 = bf16[2,32,3072]{2,1,0:T(8,128)(2,1)S(1)} collective-permute-done((bf16[2,32,3072]{2,1,0:T(8,128)(2,1)S(1)}, bf16[2,32,3072]{2,1,0:T(8,128)(2,1)S(1)}, u32[]{:S(2)}, u32[]{:S(2)}) %collective-permute-start.30) | collective-permute-done | bytes 393248 | tf_op jit(solution)/shard_map/ppermute | solution.py:275
  643.8 10.5 %collective-permute-done.60 = bf16[2,128,1024]{2,1,0:T(8,128)(2,1)S(1)} collective-permute-done((bf16[2,128,1024]{2,1,0:T(8,128)(2,1)S(1)}, bf16[2,128,1024]{2,1,0:T(8,128)(2,1)S(1)}, u32[]{:S(2)}, u32[]{:S(2)}) %collective-permute-start.60) | collective-permute-done | bytes 524320 | tf_op jit(solution)/shard_map/ppermute | solution.py:275
  672.7 11.6 %collective-permute-done.52 = bf16[32,4096]{1,0:T(8,128)(2,1)S(1)} collective-permute-done((bf16[32,4096]{1,0:T(8,128)(2,1)S(1)}, bf16[32,4096]{1,0:T(8,128)(2,1)S(1)}, u32[]{:S(2)}, u32[]{:S(2)}) %collective-permute-start.52) | collective-permute-done | bytes 262176 | tf_op jit(solution)/shard_map/ppermute | solution.py:275
  714.8 13.7 %collective-permute-done.54 = bf16[2,2,32,4096]{3,2,1,0:T(8,128)(2,1)S(1)} collective-permute-done((bf16[2,2,32,4096]{3,2,1,0:T(8,128)(2,1)S(1)}, bf16[2,2,32,4096]{3,2,1,0:T(8,128)(2,1)S(1)}, u32[]{:S(2)}, u32[]{:S(2)}) %collective-permute-start.54) | collective-permute-done | bytes 1048608 | tf_op jit(solution)/shard_map/ppermute | solution.py:275
  728.9 20.1 %collective-permute-done.64 = bf16[2,2,128,1024]{3,2,1,0:T(8,128)(2,1)S(1)} collective-permute-done((bf16[2,2,128,1024]{3,2,1,0:T(8,128)(2,1)S(1)}, bf16[2,2,128,1024]{3,2,1,0:T(8,128)(2,1)S(1)}, u32[]{:S(2)}, u32[]{:S(2)}) %collective-permute-start.64) | collective-permute-done | bytes 1048608 | tf_op jit(solution)/shard_map/ppermute | solution.py:275
  (428 shorter events, 348.9 us)
Async XLA Ops:
  7.4 37.5 %collective-permute-start.1 = (bf16[48,128]{1,0:T(8,128)(2,1)S(1)}, bf16[48,128]{1,0:T(8,128)(2,1)S(1)}, u32[]{:S(2)}, u32[]{:S(2)}) collective-permute-start(bf16[48,128]{1,0:T(8,128)(2,1)S(1)} %bitcast.373), channel_id=1, source_target_pairs={{0,1},{1,0},{2,3},{3,2},{4,5},{5,4},{6,7},{7,6},{8,9},{9,8},{10,11... | collective-permute-start | bytes 36872 | tf_op jit(solution)/shard_map/ppermute | solution.py:275
  10.4 58.4 %collective-permute-start = (bf16[512,1024]{1,0:T(8,128)(2,1)}, bf16[512,1024]{1,0:T(8,128)(2,1)}, u32[]{:S(2)}, u32[]{:S(2)}) collective-permute-start(bf16[512,1024]{1,0:T(8,128)(2,1)} %param.14), channel_id=1, source_target_pairs={{1,2},{2,1},{5,6},{6,5},{9,10},{10,9},{13,14},{14,13},{17,18},{18,... | collective-permute-start | bytes 3145736 | tf_op jit(solution)/shard_map/ppermute | solution.py:294
  14.2 54.5 %collective-permute-start.2 = (bf16[128,3072]{1,0:T(8,128)(2,1)}, bf16[128,3072]{1,0:T(8,128)(2,1)}, u32[]{:S(2)}, u32[]{:S(2)}) collective-permute-start(bf16[128,3072]{1,0:T(8,128)(2,1)} %constant_dynamic-slice_fusion.15), channel_id=1, source_target_pairs={{0,1},{1,0},{2,3},{3,2},{4,5},{5,4},{6,7},{7,6},{8,9},{9,8},{10,11... | collective-permute-start | bytes 2359304 | tf_op jit(solution)/shard_map/ppermute | solution.py:275
  16.6 41.3 %collective-permute-start.7 = (bf16[128,1024]{1,0:T(8,128)(2,1)S(1)}, bf16[128,1024]{1,0:T(8,128)(2,1)}, u32[]{:S(2)}, u32[]{:S(2)}) collective-permute-start(bf16[128,1024]{1,0:T(8,128)(2,1)S(1)} %constant_dynamic-slice_fusion.14), channel_id=1, source_target_pairs={{0,1},{1,0},{2,3},{3,2},{4,5},{5,4},{6,7},{7,6},{8,9},{9,8},{10,11... | collective-permute-start | bytes 786440 | tf_op jit(solution)/shard_map/ppermute | solution.py:275
  19.5 57.3 %collective-permute-start.10 = (bf16[128,4096]{1,0:T(8,128)(2,1)}, bf16[128,4096]{1,0:T(8,128)(2,1)}, u32[]{:S(2)}, u32[]{:S(2)}) collective-permute-start(bf16[128,4096]{1,0:T(8,128)(2,1)} %constant_dynamic-slice_fusion.13), channel_id=1, source_target_pairs={{0,1},{1,0},{2,3},{3,2},{4,5},{5,4},{6,7},{7,6},{8,9},{9,8},{10,11... | collective-permute-start | bytes 3145736 | tf_op jit(solution)/shard_map/ppermute | solution.py:275
  44.9 67.1 %collective-permute-start.17 = (bf16[512,1024]{1,0:T(8,128)(2,1)}, bf16[512,1024]{1,0:T(8,128)(2,1)}, u32[]{:S(2)}, u32[]{:S(2)}) collective-permute-start(bf16[512,1024]{1,0:T(8,128)(2,1)} %param.27), channel_id=1, source_target_pairs={{1,2},{2,1},{5,6},{6,5},{9,10},{10,9},{13,14},{14,13},{17,18},{18,... | collective-permute-start | bytes 3145736 | tf_op jit(solution)/shard_map/ppermute | solution.py:294
  64.5 40.7 %collective-permute-start.13 = (bf16[512,1024]{1,0:T(8,128)(2,1)}, bf16[512,1024]{1,0:T(8,128)(2,1)}, u32[]{:S(2)}, u32[]{:S(2)}) collective-permute-start(bf16[512,1024]{1,0:T(8,128)(2,1)} %constant_dynamic-slice_fusion.12), channel_id=1, source_target_pairs={{0,1},{1,0},{2,3},{3,2},{4,5},{5,4},{6,7},{7,6},{8,9},{9,8},{10,11... | collective-permute-start | bytes 3145736 | tf_op jit(solution)/shard_map/ppermute | solution.py:275
  68.7 38.0 %collective-permute-start.9 = (bf16[256,1024]{1,0:T(8,128)(2,1)}, bf16[256,1024]{1,0:T(8,128)(2,1)}, u32[]{:S(2)}, u32[]{:S(2)}) collective-permute-start(bf16[256,1024]{1,0:T(8,128)(2,1)} %bitcast.13), channel_id=1, source_target_pairs={{0,2},{1,3},{2,0},{3,1},{4,6},{5,7},{6,4},{7,5},{8,10},{9,11},{10,... | collective-permute-start | bytes 1572872 | tf_op jit(solution)/shard_map/ppermute | solution.py:275
  70.0 44.0 %collective-permute-start.3 = (bf16[128,3072]{1,0:T(8,128)(2,1)}, bf16[128,3072]{1,0:T(8,128)(2,1)}, u32[]{:S(2)}, u32[]{:S(2)}) collective-permute-start(bf16[128,3072]{1,0:T(8,128)(2,1)} %collective-permute-done.2), channel_id=1, source_target_pairs={{0,4},{1,5},{2,6},{3,7},{4,0},{5,1},{6,2},{7,3},{8,12},{9,13},{10,... | collective-permute-start | bytes 2359304 | tf_op jit(solution)/shard_map/ppermute | solution.py:275
  76.8 39.2 %collective-permute-start.11 = (bf16[128,4096]{1,0:T(8,128)(2,1)}, bf16[128,4096]{1,0:T(8,128)(2,1)S(1)}, u32[]{:S(2)}, u32[]{:S(2)}) collective-permute-start(bf16[128,4096]{1,0:T(8,128)(2,1)} %collective-permute-done.10), channel_id=1, source_target_pairs={{0,4},{1,5},{2,6},{3,7},{4,0},{5,1},{6,2},{7,3},{8,12},{9,13},{10,... | collective-permute-start | bytes 3145736 | tf_op jit(solution)/shard_map/ppermute | solution.py:275
  119.0 86.1 %collective-permute-start.12 = (bf16[256,4096]{1,0:T(8,128)(2,1)}, bf16[256,4096]{1,0:T(8,128)(2,1)}, u32[]{:S(2)}, u32[]{:S(2)}) collective-permute-start(bf16[256,4096]{1,0:T(8,128)(2,1)} %bitcast.16), channel_id=1, source_target_pairs={{0,2},{1,3},{2,0},{3,1},{4,6},{5,7},{6,4},{7,5},{8,10},{9,11},{10,... | collective-permute-start | bytes 6291464 | tf_op jit(solution)/shard_map/ppermute | solution.py:275
  137.1 81.6 %collective-permute-start.15 = (bf16[1024,1024]{1,0:T(8,128)(2,1)}, bf16[1024,1024]{1,0:T(8,128)(2,1)}, u32[]{:S(2)}, u32[]{:S(2)}) collective-permute-start(bf16[1024,1024]{1,0:T(8,128)(2,1)} %bitcast.19), channel_id=1, source_target_pairs={{0,2},{1,3},{2,0},{3,1},{4,6},{5,7},{6,4},{7,5},{8,10},{9,11},{10,... | collective-permute-start | bytes 6291464 | tf_op jit(solution)/shard_map/ppermute | solution.py:275
  367.7 80.3 %collective-permute-start.16 = (bf16[512,1024]{1,0:T(8,128)(2,1)}, bf16[512,1024]{1,0:T(8,128)(2,1)}, u32[]{:S(2)}, u32[]{:S(2)}) collective-permute-start(bf16[512,1024]{1,0:T(8,128)(2,1)} %add_convert_fusion.6), channel_id=1, source_target_pairs={{1,2},{2,1},{5,6},{6,5},{9,10},{10,9},{13,14},{14,13},{17,18},{18,... | collective-permute-start | bytes 3145736 | tf_op jit(solution)/shard_map/ppermute | solution.py:294
  371.0 45.1 %collective-permute-start.19 = (bf16[512,1024]{0,1:T(8,128)(2,1)}, bf16[512,1024]{0,1:T(8,128)(2,1)}, u32[]{:S(2)}, u32[]{:S(2)}) collective-permute-start(bf16[512,1024]{0,1:T(8,128)(2,1)} %bitcast.28), channel_id=1, source_target_pairs={{0,2},{1,3},{2,0},{3,1},{4,6},{5,7},{6,4},{7,5},{8,10},{9,11},{10,... | collective-permute-start | bytes 3145736 | tf_op jit(solution)/shard_map/ppermute | solution.py:275
  373.2 46.3 %collective-permute-start.18 = (bf16[512,1024]{0,1:T(8,128)(2,1)}, bf16[512,1024]{0,1:T(8,128)(2,1)}, u32[]{:S(2)}, u32[]{:S(2)}) collective-permute-start(bf16[512,1024]{0,1:T(8,128)(2,1)} %bitcast.25), channel_id=1, source_target_pairs={{0,2},{1,3},{2,0},{3,1},{4,6},{5,7},{6,4},{7,5},{8,10},{9,11},{10,... | collective-permute-start | bytes 3145736 | tf_op jit(solution)/shard_map/ppermute | solution.py:275
  409.6 66.8 %collective-permute-start.47 = (bf16[256,4096]{1,0:T(8,128)(2,1)S(1)}, bf16[256,4096]{1,0:T(8,128)(2,1)S(1)}, u32[]{:S(2)}, u32[]{:S(2)}) collective-permute-start(bf16[256,4096]{1,0:T(8,128)(2,1)S(1)} %copy-done.30), channel_id=1, source_target_pairs={{0,2},{1,3},{2,0},{3,1},{4,6},{5,7},{6,4},{7,5},{8,10},{9,11},{10,... | collective-permute-start | bytes 6291464 | tf_op jit(solution)/shard_map/ppermute | solution.py:275
  414.5 106.6 %collective-permute-start.46 = (bf16[256,4096]{1,0:T(8,128)(2,1)S(1)}, bf16[256,4096]{1,0:T(8,128)(2,1)S(1)}, u32[]{:S(2)}, u32[]{:S(2)}) collective-permute-start(bf16[256,4096]{1,0:T(8,128)(2,1)S(1)} %copy-done.28), channel_id=1, source_target_pairs={{0,2},{1,3},{2,0},{3,1},{4,6},{5,7},{6,4},{7,5},{8,10},{9,11},{10,... | collective-permute-start | bytes 6291464 | tf_op jit(solution)/shard_map/ppermute | solution.py:275
  476.4 42.2 %collective-permute-start.28 = (bf16[256,3072]{1,0:T(8,128)(2,1)}, bf16[256,3072]{1,0:T(8,128)(2,1)S(1)}, u32[]{:S(2)}, u32[]{:S(2)}) collective-permute-start(bf16[256,3072]{1,0:T(8,128)(2,1)} %add_convert_fusion.5), channel_id=1, source_target_pairs={{0,1},{1,0},{2,3},{3,2},{4,5},{5,4},{6,7},{7,6},{8,9},{9,8},{10,11... | collective-permute-start | bytes 4718600 | tf_op jit(solution)/shard_map/ppermute | solution.py:275
  479.9 83.6 %collective-permute-start.48 = (bf16[256,4096]{1,0:T(8,128)(2,1)S(1)}, bf16[256,4096]{1,0:T(8,128)(2,1)S(1)}, u32[]{:S(2)}, u32[]{:S(2)}) collective-permute-start(bf16[256,4096]{1,0:T(8,128)(2,1)S(1)} %add_convert_fusion.3), channel_id=1, source_target_pairs={{0,1},{1,0},{2,3},{3,2},{4,5},{5,4},{6,7},{7,6},{8,9},{9,8},{10,11... | collective-permute-start | bytes 6291464 | tf_op jit(solution)/shard_map/ppermute | solution.py:275
  488.7 77.5 %collective-permute-start.56 = (bf16[1024,1024]{1,0:T(8,128)(2,1)S(1)}, bf16[1024,1024]{1,0:T(8,128)(2,1)S(1)}, u32[]{:S(2)}, u32[]{:S(2)}) collective-permute-start(bf16[1024,1024]{1,0:T(8,128)(2,1)S(1)} %copy-done.49), channel_id=1, source_target_pairs={{0,2},{1,3},{2,0},{3,1},{4,6},{5,7},{6,4},{7,5},{8,10},{9,11},{10,... | collective-permute-start | bytes 6291464 | tf_op jit(solution)/shard_map/ppermute | solution.py:275
  490.5 115.2 %collective-permute-start.58 = (bf16[1024,1024]{1,0:T(8,128)(2,1)S(1)}, bf16[1024,1024]{1,0:T(8,128)(2,1)S(1)}, u32[]{:S(2)}, u32[]{:S(2)}) collective-permute-start(bf16[1024,1024]{1,0:T(8,128)(2,1)S(1)} %add_convert_fusion.1), channel_id=1, source_target_pairs={{0,1},{1,0},{2,3},{3,2},{4,5},{5,4},{6,7},{7,6},{8,9},{9,8},{10,11... | collective-permute-start | bytes 6291464 | tf_op jit(solution)/shard_map/ppermute | solution.py:275
  519.4 89.3 %collective-permute-start.29 = (bf16[2,2,32,3072]{3,2,1,0:T(8,128)(2,1)S(1)}, bf16[2,2,32,3072]{3,2,1,0:T(8,128)(2,1)S(1)}, u32[]{:S(2)}, u32[]{:S(2)}) collective-permute-start(bf16[2,2,32,3072]{3,2,1,0:T(8,128)(2,1)S(1)} %dynamic-slice_bitcast_fusion.2), channel_id=1, source_target_pairs={{0,4},{1,5},{2,6},{3,7},{4,0},{5,1},{6,2},{7,3},{8,12},{9,13},{10,... | collective-permute-start | bytes 2359304 | tf_op jit(solution)/shard_map/ppermute | solution.py:275
  564.6 45.5 %collective-permute-start.49 = (bf16[2,2,32,4096]{3,2,1,0:T(8,128)(2,1)S(1)}, bf16[2,2,32,4096]{3,2,1,0:T(8,128)(2,1)S(1)}, u32[]{:S(2)}, u32[]{:S(2)}) collective-permute-start(bf16[2,2,32,4096]{3,2,1,0:T(8,128)(2,1)S(1)} %dynamic-slice_bitcast_fusion.1), channel_id=1, source_target_pairs={{0,4},{1,5},{2,6},{3,7},{4,0},{5,1},{6,2},{7,3},{8,12},{9,13},{10,... | collective-permute-start | bytes 3145736 | tf_op jit(solution)/shard_map/ppermute | solution.py:275
  711.5 37.5 %collective-permute-start.64 = (bf16[2,2,128,1024]{3,2,1,0:T(8,128)(2,1)S(1)}, bf16[2,2,128,1024]{3,2,1,0:T(8,128)(2,1)S(1)}, u32[]{:S(2)}, u32[]{:S(2)}) collective-permute-start(bf16[2,2,128,1024]{3,2,1,0:T(8,128)(2,1)S(1)} %pad_maximum_fusion.14), channel_id=1, source_target_pairs={{0,4},{1,5},{2,6},{3,7},{4,0},{5,1},{6,2},{7,3},{8,12},{9,13},{10,... | collective-permute-start | bytes 3145736 | tf_op jit(solution)/shard_map/ppermute | solution.py:275
  (95 other events, 1237.4 us)

commit v2 on v1

--- a/solution.py
+++ b/solution.py
@@ -270,6 +270,12 @@
         self.x = (rep // 2) % 2
         self.z_low = (rep // 4) % 2
         self.z_high = rep // 8
+        self.bits = {
+            "core": (self.core, CORE_BIT),
+            "x": (self.x, X_BIT),
+            "low": (self.z_low, LOW_BIT),
+            "high": (self.z_high, HIGH_BIT),
+        }
 
     def swap(self, array, bit):
         return lax.ppermute(array, AXES, [(i, i ^ bit) for i in range(32)])
@@ -295,12 +301,15 @@
     return jnp.where(grid.y == grid.core, array, moved)
 
 
-def whole_weight(grid, own):
+def quarter_of(grid, own):
+    quarter = own.shape[0] // 4
+    place = grid.core * 2 + grid.x
+    return lax.dynamic_slice_in_dim(own, place * quarter, quarter, 0)
+
+
+def whole_weight(grid, own, first):
     rows, columns = own.shape
     quarter = rows // 4
-    place = grid.core * 2 + grid.x
-    sent = lax.dynamic_slice_in_dim(own, place * quarter, quarter, 0)
-    first = grid.swap(sent, Y_BIT)
     second = grid.swap(first, X_BIT)
     half = join(first, second, grid.x).reshape(2 * quarter, columns)
     other = grid.swap(half, CORE_BIT)
@@ -313,10 +322,9 @@
     )
 
 
-def reduced_gradient(grid, features, grads):
+def begin_sum(grid, features, grads):
     f32, bf16 = jnp.float32, jnp.bfloat16
     tok_rows, width = features.shape
-    columns = grads.shape[1]
     split = features.reshape(tok_rows, 2, 2, width // 4)
 
     def part(side, core):
@@ -328,20 +336,34 @@
     got_far = grid.swap(part(far_side, far_core).astype(bf16), CORE_BIT)
     got_near = grid.swap(part(grid.y, far_core).astype(bf16), CORE_BIT)
     far = (part(far_side, grid.core) + got_far.astype(f32)).astype(bf16)
-    got = grid.swap(far, Y_BIT)
-    total = (part(grid.y, grid.core) + got_near.astype(f32) + got.astype(f32)).astype(bf16)
-    total = total.reshape(2, 2, 2, width // 32, columns)
-    for index, bit in ((grid.x, X_BIT), (grid.z_low, LOW_BIT), (grid.z_high, HIGH_BIT)):
+    return far, (part(grid.y, grid.core) + got_near.astype(f32)).astype(bf16)
+
+
+def add_group(near, got):
+    rows, columns = near.shape
+    total = (near.astype(jnp.float32) + got.astype(jnp.float32)).astype(jnp.bfloat16)
+    return total.reshape(2, 2, 2, rows // 8, columns)
+
+
+def scatter(grid, total, names):
+    for name in names:
+        index, bit = grid.bits[name]
         got = grid.swap(half_of(total, 1 - index), bit)
-        total = (half_of(total, index).astype(f32) + got.astype(f32)).astype(bf16)
-    for index, bit in (
-        (grid.z_high, HIGH_BIT),
-        (grid.z_low, LOW_BIT),
-        (grid.x, X_BIT),
-        (grid.core, CORE_BIT),
-    ):
+        total = (half_of(total, index).astype(jnp.float32) + got.astype(jnp.float32)).astype(
+            jnp.bfloat16
+        )
+    return total
+
+
+def gather(grid, total, names):
+    for name in names:
+        index, bit = grid.bits[name]
         total = join(total, grid.swap(total, bit), index)
-    return total.reshape(width // 2, columns).astype(f32)
+    return total
+
+
+def as_rows(total):
+    return total.reshape(-1, total.shape[-1]).astype(jnp.float32)
 
 
 def summed_everywhere(grid, vector):
@@ -379,7 +401,7 @@
     return mixed.reshape(tok_rows, width).astype(bf16), logsum
 
 
-def attention_backward(query_b, keys_b, values_b, grad_mixed_b, logsum, first_row, key_pos):
+def attention_scores_backward(query_b, keys_b, values_b, grad_mixed_b, logsum, first_row, key_pos):
     f32, bf16 = jnp.float32, jnp.bfloat16
     tok_rows, width = query_b.shape
     query_heads = query_b.reshape(tok_rows, HEADS, HEAD)
@@ -394,6 +416,15 @@
     )
     row_delta = jnp.sum(attn_probs * grad_probs, axis=-1, keepdims=True)
     grad_scores_b = (attn_probs * (grad_probs - row_delta)).astype(bf16)
+    return probs_b, grad_scores_b
+
+
+def attention_products_backward(query_b, keys_b, grad_mixed_b, probs_b, grad_scores_b):
+    f32, bf16 = jnp.float32, jnp.bfloat16
+    tok_rows, width = query_b.shape
+    query_heads = query_b.reshape(tok_rows, HEADS, HEAD)
+    key_heads = keys_b.reshape(-1, HEADS, HEAD)
+    grad_mixed_heads = grad_mixed_b.reshape(tok_rows, HEADS, HEAD)
     scale = HEAD ** (-0.5)
     grad_query = (
         jnp.einsum("hqk,khd->qhd", grad_scores_b, key_heads, preferred_element_type=f32) * scale
@@ -436,10 +467,22 @@
         start += vector.shape[0]
     gain_one, shift_one, pair_bias, out_bias, gain_two, shift_two, up_bias, down_bias = full_vectors
     tokens = transpose_pairs(grid, tokens)
-    packed_w = whole_weight(grid, qkv_weight)
-    proj_w = whole_weight(grid, proj_weight)
-    up_w = whole_weight(grid, fc1_weight)
-    down_w = whole_weight(grid, fc2_weight)
+    packed_first = grid.swap(quarter_of(grid, qkv_weight), Y_BIT)
+    sent_proj, sent_up, sent_down = (
+        quarter_of(grid, weight) for weight in (proj_weight, fc1_weight, fc2_weight)
+    )
+    packed_first, sent_proj, sent_up = lax.optimization_barrier(
+        (packed_first, sent_proj, sent_up)
+    )
+    proj_first = grid.swap(sent_proj, Y_BIT)
+    up_first = grid.swap(sent_up, Y_BIT)
+    up_first, sent_down = lax.optimization_barrier((up_first, sent_down))
+    down_first = grid.swap(sent_down, Y_BIT)
+    down_first, cotangent = lax.optimization_barrier((down_first, cotangent))
+    packed_w = whole_weight(grid, qkv_weight, packed_first)
+    proj_w = whole_weight(grid, proj_weight, proj_first)
+    up_w = whole_weight(grid, fc1_weight, up_first)
+    down_w = whole_weight(grid, fc2_weight, down_first)
     cotangent = transpose_pairs(grid, cotangent)
 
     first_row = grid.core * tok_rows
@@ -461,23 +504,44 @@
     hidden = jnp.dot(normed_two_b, up_w, preferred_element_type=f32) + up_bias
     active_b = tanh_gelu(hidden).astype(bf16)
     cotan = cotangent.astype(f32)
-    grad_down = reduced_gradient(grid, active_b, cotangent)
+    down_far, down_near = begin_sum(grid, active_b, cotangent)
+    down_far, cotangent, hidden = lax.optimization_barrier((down_far, cotangent, hidden))
+    down_got = grid.swap(down_far, Y_BIT)
     grad_active = jnp.einsum("td,fd->tf", cotangent, down_w, preferred_element_type=f32)
     unused_value, gelu_back = jax.vjp(tanh_gelu, hidden)
     grad_hidden = gelu_back(grad_active)[0]
     grad_hidden_b = grad_hidden.astype(bf16)
-    grad_up = reduced_gradient(grid, normed_two_b, grad_hidden_b)
+    up_far, up_near = begin_sum(grid, normed_two_b, grad_hidden_b)
     output = resid + jnp.dot(active_b, down_w, preferred_element_type=f32) + down_bias
     output = transpose_pairs(grid, output.astype(bf16))
     grad_norm_two = jnp.einsum("tf,df->td", grad_hidden_b, up_w, preferred_element_type=f32)
     grad_resid = cotan + normal_back(grad_norm_two, scaled_two, inverse_two, gain_two)
     grad_branch_b = grad_resid.astype(bf16)
-    grad_proj = reduced_gradient(grid, mixed_b, grad_branch_b)
+    proj_far, proj_near = begin_sum(grid, mixed_b, grad_branch_b)
     grad_mixed_b = jnp.einsum(
         "te,de->td", grad_branch_b, proj_w, preferred_element_type=f32
     ).astype(bf16)
-    grad_query_b, key_terms, value_terms = attention_backward(
+    down_got, up_far, proj_far, grad_mixed_b = lax.optimization_barrier(
+        (down_got, up_far, proj_far, grad_mixed_b)
+    )
+    up_got = grid.swap(up_far, Y_BIT)
+    down_part = scatter(grid, add_group(down_near, down_got), ("x", "low"))
+    probs_b, grad_scores_b = attention_scores_backward(
         query_b, keys_b, values_b, grad_mixed_b, logsum, first_row, key_pos
+    )
+    up_got, down_part, proj_far, probs_b, grad_scores_b = lax.optimization_barrier(
+        (up_got, down_part, proj_far, probs_b, grad_scores_b)
+    )
+    proj_got = grid.swap(proj_far, Y_BIT)
+    up_part = scatter(grid, add_group(up_near, up_got), ("x", "low"))
+    down_part = gather(grid, scatter(grid, down_part, ("high",)), ("high", "low"))
+    grad_query_b, key_terms, value_terms = attention_products_backward(
+        query_b, keys_b, grad_mixed_b, probs_b, grad_scores_b
+    )
+    proj_got, up_part, down_part, grad_query_b, key_terms, value_terms = (
+        lax.optimization_barrier(
+            (proj_got, up_part, down_part, grad_query_b, key_terms, value_terms)
+        )
     )
     grad_keys_b = (
         key_terms[:tok_rows].astype(f32) + grid.swap(key_terms[tok_rows:], CORE_BIT).astype(f32)
@@ -487,7 +551,22 @@
         + grid.swap(value_terms[tok_rows:], CORE_BIT).astype(f32)
     ).astype(bf16)
     grad_packed_b = jnp.concatenate([grad_query_b, grad_keys_b, grad_values_b], axis=1)
-    grad_packed = reduced_gradient(grid, normed_one_b, grad_packed_b)
+    packed_far, packed_near = begin_sum(grid, normed_one_b, grad_packed_b)
+    packed_got = grid.swap(packed_far, Y_BIT)
+    down_part = gather(grid, down_part, ("x", "core"))
+    up_part = gather(grid, scatter(grid, up_part, ("high",)), ("high", "low"))
+    proj_part = scatter(grid, add_group(proj_near, proj_got), ("x", "low"))
+    packed_got, down_part, up_part, proj_part = lax.optimization_barrier(
+        (packed_got, down_part, up_part, proj_part)
+    )
+    grad_down = as_rows(down_part)
+    packed_part = scatter(grid, add_group(packed_near, packed_got), ("x", "low", "high"))
+    proj_part = scatter(grid, proj_part, ("high",))
+    both_columns = jnp.concatenate([packed_part, proj_part], axis=-1)
+    both_columns = gather(grid, both_columns, ("high", "low", "x", "core"))
+    grad_up = as_rows(gather(grid, up_part, ("x", "core")))
+    grad_packed = as_rows(both_columns[..., : 3 * width])
+    grad_proj = as_rows(both_columns[..., 3 * width :])
     grad_norm_one = jnp.einsum("te,de->td", grad_packed_b, packed_w, preferred_element_type=f32)
     grad_inputs = grad_resid + normal_back(grad_norm_one, scaled_one, inverse_one, gain_one)
     grad_inputs = jnp.where(

time: 774 us -> 687 us (0.89)
  waiting for transfers between devices: 287 us -> 227 us
  starting transfers between devices: 84 us -> 57.1 us
    ppermute x62 -> x58, waiting for transfers between devices: 287 us -> 227 us  [swap(): return lax.ppermute(array, AXES, [(i, i ^ bit) for i in range(32)])]
    sub x0 -> x1, matrix products: none -> 40 us  [attention_scores_backward(): grad_scores_b = (attn_probs * (grad_probs - row_delta)).astype(bf16)]
    dot_general x4 -> x3, matrix products: 61.6 us -> 29.8 us  [the longest x1 11.9 us: attention_products_backward(): jnp.einsum('hqk,khd->qhd', grad_scores_b, key_heads, preferred_element_ty...]
    ppermute x62 -> x58, starting transfers between devices: 77.8 us -> 52.1 us  [swap(): return lax.ppermute(array, AXES, [(i, i ^ bit) for i in range(32)])]
    reduce_sum x0 -> x2, other arithmetic: none -> 8.28 us  [the longest x1 8.07 us: paired_device(): jnp.sum(grad_hidden_b.astype(f32), axis=0)]
  transfers between devices with their start and end apart: 66 -> 62, of which waited for: 28 -> 27; matrix products, arithmetic and copies ran while one was open for 29% -> 55% of each run, Pallas kernels for 0% -> 0%
where the time goes in v2:
time: 687 us; the launch traced here: 677 us
  waiting for transfers between devices  227 us (33%)
  matrix products  188 us (27%)
  other arithmetic  101 us (15%)
  local copies, waits for them, and re-layouts  100 us (15%)
  starting transfers between devices  57.1 us (8%)
    ppermute x58, waiting for transfers between devices, swap(): return lax.ppermute(array, AXES, [(i, i ^ bit) for i in range(32)])  227 us
    ppermute x58, starting transfers between devices, swap(): return lax.ppermute(array, AXES, [(i, i ^ bit) for i in range(32)])  52.1 us
    sub x1, matrix products, attention_scores_backward(): grad_scores_b = (attn_probs * (grad_probs - row_delta)).astype(bf16)  40 us
    dot_general x16, matrix products, part(): return jnp.einsum('td,te->de', chosen, grads, preferred_element_type=f32)  33.7 us
    convert_element_type x1, other arithmetic, attention_scores_backward(): probs_b = attn_probs.astype(bf16)  18.6 us
    dot_general x1, matrix products, pair_scores(): jnp.einsum('qhd,khd->hqk', query_heads, key_heads, preferred_element_type...  17.6 us
    dynamic_slice x3, local copies, waits for them, and re-layouts, part(): chosen = lax.dynamic_index_in_dim(chosen, core, 1, keepdims=False)  17.2 us
    convert_element_type x4, other arithmetic, as_rows(): return total.reshape(-1, total.shape[-1]).astype(jnp.float32)  14.8 us
  transfers between devices with their start and end apart: 62, of which 27 were waited for; matrix products, arithmetic and copies ran while one was open for 55% of the time, Pallas kernels for 0%

profile of v2, /device:TPU:0, one launch (start us, length us, event | category | flops | bytes accessed | tf_op | source)
XLA Modules:
  0.0 676.5 jit_solution(12661194106312760596)
XLA Ops:
  59.3 8.5 %collective-permute-done.8 = bf16[128,1024]{1,0:T(8,128)(2,1)S(1)} collective-permute-done((bf16[128,1024]{1,0:T(8,128)(2,1)}, bf16[128,1024]{1,0:T(8,128)(2,1)S(1)}, u32[]{:S(2)}, u32[]{:S(2)}) %collective-permute-start.8) | collective-permute-done | bytes 262176 | tf_op jit(solution)/shard_map/ppermute | solution.py:281
  80.8 18.5 %collective-permute-done.11 = bf16[128,4096]{1,0:T(8,128)(2,1)S(1)} collective-permute-done((bf16[128,4096]{1,0:T(8,128)(2,1)}, bf16[128,4096]{1,0:T(8,128)(2,1)S(1)}, u32[]{:S(2)}, u32[]{:S(2)}) %collective-permute-start.11) | collective-permute-done | bytes 1048608 | tf_op jit(solution)/shard_map/ppermute | solution.py:281
  119.7 9.0 %collective-permute-done.14 = bf16[512,1024]{1,0:T(8,128)(2,1)} collective-permute-done((bf16[512,1024]{1,0:T(8,128)(2,1)}, bf16[512,1024]{1,0:T(8,128)(2,1)}, u32[]{:S(2)}, u32[]{:S(2)}) %collective-permute-start.14) | collective-permute-done | bytes 1048608 | tf_op jit(solution)/shard_map/ppermute | solution.py:281
  148.2 17.6 %fusion.81 = (f32[16,512]{1,0:T(8,128)S(1)}, f32[16,512,1024]{2,1,0:T(8,128)}) fusion(f32[512,1024]{1,0:T(8,128)} %subtract_convert_fusion, f32[16]{0:T(128)S(1)} %multiply_power_fusion, bf16[512,16,64]{0,2,1:T(8,128)(2,1)} %bitcast.328, bf16[1024,16,64]{0,2,1:T(8,128)(2,1)S(1)} %bitcast.314, pred[512,1024]{1,0:T(8,128)(4,1)} %broadcast_compare_fusion), kind=kOutput, calls=%fused_computation.305 | convolution fusion | flops 1115676672 | bytes 39354432 | tf_op jit(solution)/shard_map/qhd,khd->hqk/dot_general | solution.py:377
  165.8 14.4 %fusion.2 = f32[16,512]{1,0:T(8,128)S(1)} fusion(f32[16,512,1024]{2,1,0:T(8,128)} %get-tuple-element.156, f32[16,512]{1,0:T(8,128)S(1)} %get-tuple-element.155), kind=kLoop, calls=%fused_computation.8 | loop fusion | flops 16769024 | bytes 33619968 | tf_op jit(solution)/shard_map/reduce_sum | solution.py:397
  180.3 12.9 %fusion.44 = bf16[16,64,512]{2,1,0:T(8,128)(2,1)S(1)} fusion(bf16[1024,16,64]{0,2,1:T(8,128)(2,1)S(1)} %bitcast.344, f32[16,512,1024]{2,1,0:T(8,128)} %get-tuple-element.156, f32[16,512]{1,0:T(8,128)S(1)} %fusion.2, f32[16,512]{1,0:T(8,128)S(1)} %get-tuple-element.155), kind=kOutput, calls=%fused_computation.120 | convolution fusion | flops 1099431936 | bytes 36765696 | tf_op jit(solution)/shard_map/hqk,khd->qhd/dot_general | solution.py:400
  203.9 18.6 %fusion.3 = bf16[16,512,1024]{2,1,0:T(8,128)(2,1)} fusion(f32[16,512,1024]{2,1,0:T(8,128)} %get-tuple-element.156, f32[16,512]{1,0:T(8,128)S(1)} %log_add_fusion), kind=kLoop, calls=%fused_computation.9 | loop fusion | flops 16777216 | bytes 50364416 | tf_op jit(solution)/shard_map/convert_element_type | solution.py:413
  225.7 12.8 %fusion.22 = (bf16[512,4096]{1,0:T(8,128)(2,1)}, f32[512,4096]{1,0:T(8,128)}) fusion(f32[4096]{0:T(1024)S(1)} %bitcast.361, bf16[512,1024]{1,0:T(8,128)(2,1)S(1)} %copy-done.16, bf16[1024,4096]{1,0:T(8,128)(2,1)} %constant_dynamic-update-slice_fusion.3), kind=kOutput, calls=%fused_computation.29 | convolution fusion | flops 4315938816 | bytes 22036480 | tf_op jit(solution)/shard_map/dot_general | solution.py:504
  246.4 10.5 %constant_dynamic-slice_fusion.7 = (bf16[512,1,1,1024]{3,2,1,0:T(2,128)(2,1)S(1)}, bf16[512,1,1,1024]{3,2,1,0:T(2,128)(2,1)S(1)}, bf16[512,1,1,1024]{3,2,1,0:T(2,128)(2,1)S(1)}, bf16[512,1,1,1024]{3,2,1,0:T(2,128)(2,1)S(1)}) fusion(bf16[512,2,2,1024]{3,2,1,0:T(2,128)(2,1)} %reshape.314, s32[]{:T(128)S(6)} %select_n.420, s32[]{:T(128)S(6)} %select_n.416, ...), kind=kLoop, calls=%fused_computation.238 | loop fusion | bytes 8388624 | tf_op jit(solution)/shard_map/jit(dynamic_index_in_dim)/dynamic_slice | solution.py:332
  277.7 10.5 %fusion.84 = f32[512,4096]{1,0:T(8,128)} fusion(bf16[512,1024]{1,0:T(8,128)(2,1)S(1)} %copy-done.23, bf16[4096,1024]{1,0:T(8,128)(2,1)} %constant_dynamic-update-slice_fusion), kind=kOutput, calls=%fused_computation.308 | convolution fusion | flops 4294967296 | bytes 17825792 | tf_op jit(solution)/shard_map/td,fd->tf/dot_general | solution.py:510
  288.2 8.1 %convert_reduce_fusion = (f32[4096]{0:T(1024)S(1)}, bf16[512,4096]{1,0:T(8,128)(2,1)S(1)}) fusion(f32[512,4096]{1,0:T(8,128)S(1)} %bitcast.321, f32[512,4096]{1,0:T(8,128)} %fusion.84), kind=kLoop, calls=%fused_computation.30 | loop fusion | flops 46133248 | bytes 20987904 | tf_op jit(solution)/shard_map/reduce_sum | solution.py:585
  296.2 8.0 %multiply_reduce_fusion.1 = (f32[1024]{0:T(1024)S(1)}, f32[512]{0:T(512)S(1)}, f32[512]{0:T(512)S(1)}, f32[1024]{0:T(1024)S(1)}, f32[512,1024]{1,0:T(8,128)S(1)}) fusion(f32[512,1024]{1,0:T(8,128)S(1)} %get-tuple-element.158, f32[512]{0:T(512)S(1)} %add_rsqrt_fusion, f32[512]{0:T(512)S(1)} %broadcast_multiply_fusion.4, f32[1024]{0:T(1024)S(1)} %bitcast.355, ...), kind=kOutput, calls=%fused_computation.97 | convolution fusion | flops 4299682816 | bytes 16797696 | tf_op jit(solution)/shard_map/tf,df->td/dot_general | solution.py:517
  322.0 33.6 %collective-permute-done.19 = bf16[1024,1024]{1,0:T(8,128)(2,1)S(1)} collective-permute-done((bf16[1024,1024]{1,0:T(8,128)(2,1)S(1)}, bf16[1024,1024]{1,0:T(8,128)(2,1)S(1)}, u32[]{:S(2)}, u32[]{:S(2)}) %collective-permute-start.19) | collective-permute-done | bytes 2097184 | tf_op jit(solution)/shard_map/ppermute | solution.py:281
  372.3 10.2 %collective-permute-done.24 = bf16[2,2,128,1024]{3,2,1,0:T(8,128)(2,1)} collective-permute-done((bf16[2,2,128,1024]{3,2,1,0:T(8,128)(2,1)}, bf16[2,2,128,1024]{3,2,1,0:T(8,128)(2,1)}, u32[]{:S(2)}, u32[]{:S(2)}) %collective-permute-start.24) | collective-permute-done | bytes 1048608 | tf_op jit(solution)/shard_map/ppermute | solution.py:281
  386.8 40.0 %multiply_convert_fusion = bf16[16,512,1024]{2,1,0:T(8,128)(2,1)} fusion(f32[16,512,1024]{2,1,0:T(8,128)} %get-tuple-element.156, f32[16,512]{1,0:T(8,128)S(1)} %log_add_fusion, bf16[512,16,64]{0,2,1:T(8,128)(2,1)} %bitcast.330, bf16[1024,16,64]{0,2,1:T(8,128)(2,1)} %bitcast.343), kind=kOutput, calls=%fused_computation.1 | convolution fusion | flops 2197824512 | bytes 53510144 | tf_op jit(solution)/shard_map/sub | solution.py:418
  438.0 11.9 %multiply_convert_fusion.2 = bf16[16,64,512]{2,1,0:T(8,128)(2,1)} fusion(bf16[1024,16,64]{0,2,1:T(8,128)(2,1)S(1)} %bitcast.315, bf16[16,512,1024]{2,1,0:T(8,128)(2,1)} %multiply_convert_fusion), kind=kOutput, calls=%fused_computation.104 | convolution fusion | flops 1074790400 | bytes 19922944 | tf_op jit(solution)/shard_map/hqk,khd->qhd/dot_general | solution.py:430
  451.5 9.1 %multiply_convert_fusion.1 = bf16[16,64,1024]{2,1,0:T(8,128)(2,1)S(1)} fusion(bf16[512,16,64]{0,2,1:T(8,128)(2,1)} %bitcast.329, bf16[16,512,1024]{2,1,0:T(8,128)(2,1)} %multiply_convert_fusion), kind=kOutput, calls=%fused_computation.40 | convolution fusion | flops 1075838976 | bytes 19922944 | tf_op jit(solution)/shard_map/hqk,qhd->khd/dot_general | solution.py:433
  467.2 8.8 %convolution_convert_fusion.4 = bf16[16,64,1024]{2,1,0:T(8,128)(2,1)S(1)} fusion(bf16[512,16,64]{0,2,1:T(8,128)(2,1)S(1)} %bitcast.331, bf16[16,512,1024]{2,1,0:T(8,128)(2,1)} %fusion.3), kind=kOutput, calls=%fused_computation.111 | convolution fusion | flops 1074790400 | bytes 19922944 | tf_op jit(solution)/shard_map/hqk,qhd->khd/dot_general | solution.py:435
  478.6 9.4 %collective-permute-done.29 = bf16[2,32,4096]{2,1,0:T(8,128)(2,1)S(1)} collective-permute-done((bf16[2,32,4096]{2,1,0:T(8,128)(2,1)S(1)}, bf16[2,32,4096]{2,1,0:T(8,128)(2,1)S(1)}, u32[]{:S(2)}, u32[]{:S(2)}) %collective-permute-start.29) | collective-permute-done | bytes 524320 | tf_op jit(solution)/shard_map/ppermute | solution.py:281
  492.7 10.9 %collective-permute-done.46 = bf16[32,4096]{1,0:T(8,128)(2,1)S(1)} collective-permute-done((bf16[32,4096]{1,0:T(8,128)(2,1)S(1)}, bf16[32,4096]{1,0:T(8,128)(2,1)S(1)}, u32[]{:S(2)}, u32[]{:S(2)}) %collective-permute-start.46) | collective-permute-done | bytes 262176 | tf_op jit(solution)/shard_map/ppermute | solution.py:281
  543.7 34.0 %collective-permute-done.37 = f32[96,128]{1,0:T(8,128)S(1)} collective-permute-done((f32[96,128]{1,0:T(8,128)S(1)}, f32[96,128]{1,0:T(8,128)S(1)}, u32[]{:S(2)}, u32[]{:S(2)}) %collective-permute-start.37) | collective-permute-done | bytes 49184 | tf_op jit(solution)/shard_map/ppermute | solution.py:281
  591.6 9.2 %collective-permute-done.52 = bf16[2,2,32,3072]{3,2,1,0:T(8,128)(2,1)S(1)} collective-permute-done((bf16[2,2,32,3072]{3,2,1,0:T(8,128)(2,1)S(1)}, bf16[2,2,32,3072]{3,2,1,0:T(8,128)(2,1)S(1)}, u32[]{:S(2)}, u32[]{:S(2)}) %collective-permute-start.52) | collective-permute-done | bytes 786464 | tf_op jit(solution)/shard_map/ppermute | solution.py:281
  634.0 11.2 %collective-permute-done.60 = bf16[2,2,32,4096]{3,2,1,0:T(8,128)(2,1)S(1)} collective-permute-done((bf16[2,2,32,4096]{3,2,1,0:T(8,128)(2,1)S(1)}, bf16[2,2,32,4096]{3,2,1,0:T(8,128)(2,1)S(1)}, u32[]{:S(2)}, u32[]{:S(2)}) %collective-permute-start.60) | collective-permute-done | bytes 1048608 | tf_op jit(solution)/shard_map/ppermute | solution.py:281
  651.2 12.9 %collective-permute-done.58 = bf16[2,2,32,4096]{3,2,1,0:T(8,128)(2,1)S(1)} collective-permute-done((bf16[2,2,32,4096]{3,2,1,0:T(8,128)(2,1)S(1)}, bf16[2,2,32,4096]{3,2,1,0:T(8,128)(2,1)S(1)}, u32[]{:S(2)}, u32[]{:S(2)}) %collective-permute-start.58) | collective-permute-done | bytes 1048608 | tf_op jit(solution)/shard_map/ppermute | solution.py:281
  (412 shorter events, 323.3 us)
Async XLA Ops:
  7.4 35.0 %collective-permute-start.1 = (bf16[48,128]{1,0:T(8,128)(2,1)S(1)}, bf16[48,128]{1,0:T(8,128)(2,1)S(1)}, u32[]{:S(2)}, u32[]{:S(2)}) collective-permute-start(bf16[48,128]{1,0:T(8,128)(2,1)S(1)} %bitcast.362), channel_id=1, source_target_pairs={{0,1},{1,0},{2,3},{3,2},{4,5},{5,4},{6,7},{7,6},{8,9},{9,8},{10,11... | collective-permute-start | bytes 36872 | tf_op jit(solution)/shard_map/ppermute | solution.py:281
  10.4 36.5 %collective-permute-start = (bf16[512,1024]{1,0:T(8,128)(2,1)}, bf16[512,1024]{1,0:T(8,128)(2,1)S(1)}, u32[]{:S(2)}, u32[]{:S(2)}) collective-permute-start(bf16[512,1024]{1,0:T(8,128)(2,1)} %param.14), channel_id=1, source_target_pairs={{1,2},{2,1},{5,6},{6,5},{9,10},{10,9},{13,14},{14,13},{17,18},{18,... | collective-permute-start | bytes 3145736 | tf_op jit(solution)/shard_map/ppermute | solution.py:300
  12.4 30.9 %collective-permute-start.2 = (bf16[128,3072]{1,0:T(8,128)(2,1)S(1)}, bf16[128,3072]{1,0:T(8,128)(2,1)}, u32[]{:S(2)}, u32[]{:S(2)}) collective-permute-start(bf16[128,3072]{1,0:T(8,128)(2,1)S(1)} %constant_dynamic-slice_fusion.15), channel_id=1, source_target_pairs={{0,1},{1,0},{2,3},{3,2},{4,5},{5,4},{6,7},{7,6},{8,9},{9,8},{10,11... | collective-permute-start | bytes 2359304 | tf_op jit(solution)/shard_map/ppermute | solution.py:281
  43.4 31.8 %collective-permute-start.3 = (bf16[128,3072]{1,0:T(8,128)(2,1)}, bf16[128,3072]{1,0:T(8,128)(2,1)}, u32[]{:S(2)}, u32[]{:S(2)}) collective-permute-start(bf16[128,3072]{1,0:T(8,128)(2,1)} %collective-permute-done.2), channel_id=1, source_target_pairs={{0,4},{1,5},{2,6},{3,7},{4,0},{5,1},{6,2},{7,3},{8,12},{9,13},{10,... | collective-permute-start | bytes 2359304 | tf_op jit(solution)/shard_map/ppermute | solution.py:281
  44.9 29.9 %collective-permute-start.10 = (bf16[128,4096]{1,0:T(8,128)(2,1)}, bf16[128,4096]{1,0:T(8,128)(2,1)}, u32[]{:S(2)}, u32[]{:S(2)}) collective-permute-start(bf16[128,4096]{1,0:T(8,128)(2,1)} %constant_dynamic-slice_fusion.13), channel_id=1, source_target_pairs={{0,1},{1,0},{2,3},{3,2},{4,5},{5,4},{6,7},{7,6},{8,9},{9,8},{10,11... | collective-permute-start | bytes 3145736 | tf_op jit(solution)/shard_map/ppermute | solution.py:281
  76.8 30.5 %collective-permute-start.4 = (bf16[256,3072]{1,0:T(8,128)(2,1)S(1)}, bf16[256,3072]{1,0:T(8,128)(2,1)S(1)}, u32[]{:S(2)}, u32[]{:S(2)}) collective-permute-start(bf16[256,3072]{1,0:T(8,128)(2,1)S(1)} %bitcast.324), channel_id=1, source_target_pairs={{0,2},{1,3},{2,0},{3,1},{4,6},{5,7},{6,4},{7,5},{8,10},{9,11},{10,... | collective-permute-start | bytes 4718600 | tf_op jit(solution)/shard_map/ppermute | solution.py:281
  102.3 120.2 %collective-permute-start.12 = (bf16[256,4096]{1,0:T(8,128)(2,1)}, bf16[256,4096]{1,0:T(8,128)(2,1)}, u32[]{:S(2)}, u32[]{:S(2)}) collective-permute-start(bf16[256,4096]{1,0:T(8,128)(2,1)} %bitcast.16), channel_id=1, source_target_pairs={{0,2},{1,3},{2,0},{3,1},{4,6},{5,7},{6,4},{7,5},{8,10},{9,11},{10,... | collective-permute-start | bytes 6291464 | tf_op jit(solution)/shard_map/ppermute | solution.py:281
  105.5 29.5 %collective-permute-start.17 = (bf16[512,1024]{1,0:T(8,128)(2,1)}, bf16[512,1024]{1,0:T(8,128)(2,1)}, u32[]{:S(2)}, u32[]{:S(2)}) collective-permute-start(bf16[512,1024]{1,0:T(8,128)(2,1)} %param.27), channel_id=1, source_target_pairs={{1,2},{2,1},{5,6},{6,5},{9,10},{10,9},{13,14},{14,13},{17,18},{18,... | collective-permute-start | bytes 3145736 | tf_op jit(solution)/shard_map/ppermute | solution.py:300
  131.9 130.0 %collective-permute-start.15 = (bf16[1024,1024]{1,0:T(8,128)(2,1)}, bf16[1024,1024]{1,0:T(8,128)(2,1)}, u32[]{:S(2)}, u32[]{:S(2)}) collective-permute-start(bf16[1024,1024]{1,0:T(8,128)(2,1)} %bitcast.19), channel_id=1, source_target_pairs={{0,2},{1,3},{2,0},{3,1},{4,6},{5,7},{6,4},{7,5},{8,10},{9,11},{10,... | collective-permute-start | bytes 6291464 | tf_op jit(solution)/shard_map/ppermute | solution.py:281
  261.9 53.0 %collective-permute-start.23 = (bf16[1024,1024]{1,0:T(8,128)(2,1)}, bf16[1024,1024]{1,0:T(8,128)(2,1)}, u32[]{:S(2)}, u32[]{:S(2)}) collective-permute-start(bf16[1024,1024]{1,0:T(8,128)(2,1)} %convolution_convert_fusion.5), channel_id=1, source_target_pairs={{0,2},{1,3},{2,0},{3,1},{4,6},{5,7},{6,4},{7,5},{8,10},{9,11},{10,... | collective-permute-start | bytes 6291464 | tf_op jit(solution)/shard_map/ppermute | solution.py:281
  273.1 90.5 %collective-permute-start.16 = (bf16[512,1024]{1,0:T(8,128)(2,1)S(1)}, bf16[512,1024]{1,0:T(8,128)(2,1)}, u32[]{:S(2)}, u32[]{:S(2)}) collective-permute-start(bf16[512,1024]{1,0:T(8,128)(2,1)S(1)} %add_convert_fusion.11), channel_id=1, source_target_pairs={{1,2},{2,1},{5,6},{6,5},{9,10},{10,9},{13,14},{14,13},{17,18},{18,... | collective-permute-start | bytes 3145736 | tf_op jit(solution)/shard_map/ppermute | solution.py:300
  307.9 47.7 %collective-permute-start.19 = (bf16[1024,1024]{1,0:T(8,128)(2,1)S(1)}, bf16[1024,1024]{1,0:T(8,128)(2,1)S(1)}, u32[]{:S(2)}, u32[]{:S(2)}) collective-permute-start(bf16[1024,1024]{1,0:T(8,128)(2,1)S(1)} %copy-done.46), channel_id=1, source_target_pairs={{0,1},{1,0},{2,3},{3,2},{4,5},{5,4},{6,7},{7,6},{8,9},{9,8},{10,11... | collective-permute-start | bytes 6291464 | tf_op jit(solution)/shard_map/ppermute | solution.py:281
  361.9 65.1 %collective-permute-start.27 = (bf16[256,4096]{1,0:T(8,128)(2,1)}, bf16[256,4096]{1,0:T(8,128)(2,1)}, u32[]{:S(2)}, u32[]{:S(2)}) collective-permute-start(bf16[256,4096]{1,0:T(8,128)(2,1)} %convolution_convert_fusion), channel_id=1, source_target_pairs={{0,2},{1,3},{2,0},{3,1},{4,6},{5,7},{6,4},{7,5},{8,10},{9,11},{10,... | collective-permute-start | bytes 6291464 | tf_op jit(solution)/shard_map/ppermute | solution.py:281
  363.1 127.1 %collective-permute-start.49 = (bf16[256,1024]{1,0:T(8,128)(2,1)}, bf16[256,1024]{1,0:T(8,128)(2,1)}, u32[]{:S(2)}, u32[]{:S(2)}) collective-permute-start(bf16[256,1024]{1,0:T(8,128)(2,1)} %convolution_convert_fusion.8), channel_id=1, source_target_pairs={{0,2},{1,3},{2,0},{3,1},{4,6},{5,7},{6,4},{7,5},{8,10},{9,11},{10,... | collective-permute-start | bytes 1572872 | tf_op jit(solution)/shard_map/ppermute | solution.py:281
  368.1 58.9 %collective-permute-start.22 = (bf16[256,4096]{1,0:T(8,128)(2,1)}, bf16[256,4096]{1,0:T(8,128)(2,1)}, u32[]{:S(2)}, u32[]{:S(2)}) collective-permute-start(bf16[256,4096]{1,0:T(8,128)(2,1)} %add_convert_fusion.4), channel_id=1, source_target_pairs={{0,1},{1,0},{2,3},{3,2},{4,5},{5,4},{6,7},{7,6},{8,9},{9,8},{10,11... | collective-permute-start | bytes 6291464 | tf_op jit(solution)/shard_map/ppermute | solution.py:281
  385.1 41.6 %collective-permute-start.25 = (bf16[2,128,1024]{2,1,0:T(8,128)(2,1)S(1)}, bf16[2,128,1024]{2,1,0:T(8,128)(2,1)S(1)}, u32[]{:S(2)}, u32[]{:S(2)}) collective-permute-start(bf16[2,128,1024]{2,1,0:T(8,128)(2,1)S(1)} %dynamic-slice_bitcast_fusion.4), channel_id=1, source_target_pairs={{0,8},{1,9},{2,10},{3,11},{4,12},{5,13},{6,14},{7,15},{8,0},{9,1},... | collective-permute-start | bytes 1572872 | tf_op jit(solution)/shard_map/ppermute | solution.py:281
  433.9 29.7 %collective-permute-start.28 = (bf16[2,2,32,4096]{3,2,1,0:T(8,128)(2,1)}, bf16[2,2,32,4096]{3,2,1,0:T(8,128)(2,1)}, u32[]{:S(2)}, u32[]{:S(2)}) collective-permute-start(bf16[2,2,32,4096]{3,2,1,0:T(8,128)(2,1)} %dynamic-slice_bitcast_fusion), channel_id=1, source_target_pairs={{0,4},{1,5},{2,6},{3,7},{4,0},{5,1},{6,2},{7,3},{8,12},{9,13},{10,... | collective-permute-start | bytes 3145736 | tf_op jit(solution)/shard_map/ppermute | solution.py:281
  488.3 30.0 %collective-permute-start.34 = (bf16[512,1024]{0,1:T(8,128)(2,1)S(1)}, bf16[512,1024]{0,1:T(8,128)(2,1)S(1)}, u32[]{:S(2)}, u32[]{:S(2)}) collective-permute-start(bf16[512,1024]{0,1:T(8,128)(2,1)S(1)} %slice.123), channel_id=1, source_target_pairs={{0,2},{1,3},{2,0},{3,1},{4,6},{5,7},{6,4},{7,5},{8,10},{9,11},{10,... | collective-permute-start | bytes 3145736 | tf_op jit(solution)/shard_map/ppermute | solution.py:281
  488.5 30.2 %collective-permute-start.33 = (bf16[512,1024]{0,1:T(8,128)(2,1)S(1)}, bf16[512,1024]{0,1:T(8,128)(2,1)S(1)}, u32[]{:S(2)}, u32[]{:S(2)}) collective-permute-start(bf16[512,1024]{0,1:T(8,128)(2,1)S(1)} %slice.121), channel_id=1, source_target_pairs={{0,2},{1,3},{2,0},{3,1},{4,6},{5,7},{6,4},{7,5},{8,10},{9,11},{10,... | collective-permute-start | bytes 3145736 | tf_op jit(solution)/shard_map/ppermute | solution.py:281
  531.9 50.4 %collective-permute-start.45 = (bf16[2,2,2,128,1024]{4,3,2,1,0:T(8,128)(2,1)S(1)}, bf16[2,2,2,128,1024]{4,3,2,1,0:T(8,128)(2,1)S(1)}, u32[]{:S(2)}, u32[]{:S(2)}) collective-permute-start(bf16[2,2,2,128,1024]{4,3,2,1,0:T(8,128)(2,1)S(1)} %pad_maximum_fusion.7), channel_id=1, source_target_pairs={{0,2},{1,3},{2,0},{3,1},{4,6},{5,7},{6,4},{7,5},{8,10},{9,11},{10,... | collective-permute-start | bytes 6291464 | tf_op jit(solution)/shard_map/ppermute | solution.py:281
  533.8 49.2 %collective-permute-start.41 = (bf16[256,3072]{1,0:T(8,128)(2,1)S(1)}, bf16[256,3072]{1,0:T(8,128)(2,1)S(1)}, u32[]{:S(2)}, u32[]{:S(2)}) collective-permute-start(bf16[256,3072]{1,0:T(8,128)(2,1)S(1)} %convolution_convert_fusion.3), channel_id=1, source_target_pairs={{0,2},{1,3},{2,0},{3,1},{4,6},{5,7},{6,4},{7,5},{8,10},{9,11},{10,... | collective-permute-start | bytes 4718600 | tf_op jit(solution)/shard_map/ppermute | solution.py:281
  540.5 42.4 %collective-permute-start.43 = (bf16[256,3072]{1,0:T(8,128)(2,1)S(1)}, bf16[256,3072]{1,0:T(8,128)(2,1)S(1)}, u32[]{:S(2)}, u32[]{:S(2)}) collective-permute-start(bf16[256,3072]{1,0:T(8,128)(2,1)S(1)} %add_convert_fusion.7), channel_id=1, source_target_pairs={{0,1},{1,0},{2,3},{3,2},{4,5},{5,4},{6,7},{7,6},{8,9},{9,8},{10,11... | collective-permute-start | bytes 4718600 | tf_op jit(solution)/shard_map/ppermute | solution.py:281
  541.7 36.0 %collective-permute-start.37 = (f32[96,128]{1,0:T(8,128)S(1)}, f32[96,128]{1,0:T(8,128)S(1)}, u32[]{:S(2)}, u32[]{:S(2)}) collective-permute-start(f32[96,128]{1,0:T(8,128)S(1)} %bitcast_add_fusion), channel_id=1, source_target_pairs={{0,1},{1,0},{2,3},{3,2},{4,5},{5,4},{6,7},{7,6},{8,9},{9,8},{10,11... | collective-permute-start | bytes 147464 | tf_op jit(solution)/shard_map/ppermute | solution.py:281
  587.4 34.9 %collective-permute-start.35 = (bf16[512,1024]{1,0:T(8,128)(2,1)S(1)}, bf16[512,1024]{1,0:T(8,128)(2,1)S(1)}, u32[]{:S(2)}, u32[]{:S(2)}) collective-permute-start(bf16[512,1024]{1,0:T(8,128)(2,1)S(1)} %get-tuple-element.89), channel_id=1, source_target_pairs={{1,2},{2,1},{5,6},{6,5},{9,10},{10,9},{13,14},{14,13},{17,18},{18,... | collective-permute-start | bytes 3145736 | tf_op jit(solution)/shard_map/ppermute | solution.py:300
  (89 other events, 1065.0 us)
